TPU v7x, 128 devices: a whole 4x4x4 slice. The times are simulated.
128 devices in a mesh: tm: 64 (over x, y, z), space: 2 (over core).
Axes of the slice: x: 4, y: 4, z: 4, core: 2. Of those that a mesh axis runs over, the one named last changes fastest.
Arguments:
- clean: bfloat16 [320, 16, 16, 1280], P('tm', 'space'), may hold values from -6 to 6
- noise: bfloat16 [320, 16, 16, 1280], P('tm', 'space'), may hold values from -6 to 6
- timestep: int32 [1], replicated, may hold values from 0 to 999
- spatial_weight: bfloat16 [1280, 3, 3, 640], replicated, may hold values from -0.0546875 to 0.0546875
- temporal_weight: bfloat16 [640, 3, 640], replicated, may hold values from -0.125 to 0.125
Outputs:
- loss: float32 [], replicated
- spatial_grad: float32 [1280, 3, 3, 640], P(('tm', 'space'))
- temporal_grad: float32 [640, 3, 640], P(('tm', 'space'))
All inputs are finite; a program needn't handle non-finite values.
Results may differ from a plain program's by a relative error of at most 0.0036.
Values may be sent and summed in bfloat16 or wider, within the bound.
No kernel may reach another device: no remote copies, remote signals or barrier semaphores. Data moves between devices by JAX's collectives and lax.ppermute only.
A program may use at most 256 MiB of HBM per device.

v0:
```python
import functools
import math

import jax
import jax.numpy as jnp
import numpy as np
from jax import lax
from jax.experimental import pallas as pl
from jax.experimental.pallas import tpu as pltpu
from jax.sharding import PartitionSpec as P

CLIP = 80
STEPS = 1000
BF = jnp.bfloat16
F32 = jnp.float32
MIB = 1 << 20
STRIDES = (16, 4, 1)
RING = 4
ORDERS = ((0, 1, 2), (1, 2, 0), (2, 0, 1))
LOSS = 16
EXTRA = 64


def params(mib):
    return pltpu.CompilerParams(vmem_limit_bytes=mib * MIB)


def in_hbm(x):
    return pltpu.with_memory_space_constraint(x, pltpu.HBM)


def in_vmem(x):
    return pltpu.with_memory_space_constraint(x, pltpu.VMEM)


def cost(flops, nbytes):
    return pl.CostEstimate(flops=int(flops), bytes_accessed=int(nbytes), transcendentals=0)


def spatial_forward_kernel(
    odd, x_ref, above_ref, below_ref, w_ref, act_ref, one_ref, two_ref, der_ref, xp, acc, taps, sems
):
    order = (1, 0, 2)
    step = pl.program_id(0)
    first = jnp.where(step == 0, 1, jnp.where(step == 1, 0, 2))
    frames, span, channels = x_ref.shape
    cols = above_ref.shape[1]
    features = w_ref.shape[3]
    wide = features // 256 * 256
    rest = features - wide

    @pl.when(step == 0)
    def _():
        for k in range(9):
            pltpu.make_async_copy(w_ref.at[order[k // 3], k % 3], taps.at[k], sems.at[k]).start()
        xp[:, 0:cols, :] = above_ref[...]
        xp[:, cols : cols + span, :] = x_ref[...]
        xp[:, cols + span : span + 2 * cols, :] = below_ref[...]
        acc[...] = jnp.zeros_like(acc)

    start = pl.multiple_of(first * cols, cols)
    piece = xp[:, pl.ds(start, span), :].reshape(frames * span, channels)
    for b in range(3):
        k = 3 * step + b
        pltpu.make_async_copy(w_ref.at[first, b], taps.at[k], sems.at[k]).wait()
        acc[b, :, 0:wide] += jnp.dot(piece, taps[k, :, 0:wide], preferred_element_type=F32)
    ends = jnp.concatenate([taps[3 * step + b, :, wide:] for b in range(3)], axis=1)
    prod = jnp.dot(piece, ends, preferred_element_type=F32)
    for b in range(3):
        acc[b, :, wide:] += prod[:, b * rest : (b + 1) * rest]

    @pl.when(step == 2)
    def _():
        col = lax.broadcasted_iota(jnp.int32, (span, features), 0) % cols

        def one(f, carry):
            rows = pl.ds(pl.multiple_of(f * span, span), span)
            left = jnp.where(col == 0, 0.0, pltpu.roll(acc[0, rows, :], 1, 0))
            right = jnp.where(col == cols - 1, 0.0, pltpu.roll(acc[2, rows, :], span - 1, 0))
            hidden = left + acc[1, rows, :] + right
            sig = 1.0 / (1.0 + jnp.exp(-hidden))
            act_ref[f] = (hidden * sig).astype(BF)
            der_ref[f] = sig * (1.0 + hidden * (1.0 - sig))
            return carry

        lax.fori_loop(0, frames, one, 0)
        one_ref[0] = act_ref[(1 - odd[0]) * (frames - 1)]
        two_ref[0] = act_ref[odd[0] * (frames - 1)]


def spatial_forward(odd, x, above, below, weight):
    frames, span, channels = x.shape
    cols = above.shape[1]
    features = weight.shape[3]
    whole = lambda s: (0, 0, 0)
    return pl.pallas_call(
        spatial_forward_kernel,
        grid=(3,),
        in_specs=[
            pl.BlockSpec(memory_space=pltpu.SMEM),
            pl.BlockSpec(x.shape, whole),
            pl.BlockSpec(above.shape, whole),
            pl.BlockSpec(below.shape, whole),
            pl.BlockSpec(memory_space=pltpu.HBM),
        ],
        out_specs=[
            pl.BlockSpec((frames, span, features), whole),
            pl.BlockSpec((1, span, features), whole),
            pl.BlockSpec((1, span, features), whole),
            pl.BlockSpec((frames, span, features), whole),
        ],
        out_shape=[
            jax.ShapeDtypeStruct((frames, span, features), BF),
            jax.ShapeDtypeStruct((1, span, features), BF),
            jax.ShapeDtypeStruct((1, span, features), BF),
            pltpu.VMEM((frames, span, features), F32),
        ],
        scratch_shapes=[
            pltpu.VMEM((frames, span + 2 * cols, channels), BF),
            pltpu.VMEM((3, frames * span, features), F32),
            pltpu.VMEM((9, channels, features), BF),
            pltpu.SemaphoreType.DMA((9,)),
        ],
        compiler_params=params(40),
        cost_estimate=cost(
            2 * 9 * frames * span * channels * features, 2 * 9 * channels * features
        ),
        name="spatial_forward",
    )(odd, x, above, below, in_hbm(weight))


def temporal_forward_kernel(
    scale, odd, act_ref, one_ref, two_ref, w_ref, clean_ref, noise_ref, *rest
):
    gp_ref, one_out, two_out, loss_ref, rim_ref, ap = rest[1:]
    frames, span, features = act_ref.shape
    factor = scale[2]
    ap[(1 - odd[0]) * (frames + 1)] = one_ref[0]
    ap[odd[0] * (frames + 1)] = two_ref[0]
    ap[1 : frames + 1] = act_ref[...]
    pred = jnp.zeros((frames * span, features), F32)
    for tap in range(3):
        pred = pred + jnp.dot(
            ap[tap : tap + frames].reshape(frames * span, features),
            w_ref[tap],
            preferred_element_type=F32,
        )
    clean = clean_ref[...].reshape(frames * span, features).astype(F32)
    noise = noise_ref[...].reshape(frames * span, features).astype(F32)
    diff = pred - (scale[0] * noise - scale[1] * clean)
    gp_ref[...] = (2.0 * diff / factor).astype(BF).reshape(frames, span, features)
    one_out[0] = gp_ref[(1 - odd[0]) * (frames - 1)]
    two_out[0] = gp_ref[odd[0] * (frames - 1)]
    loss = jnp.sum(diff * diff, axis=0, keepdims=True)
    loss_ref[...] = loss
    rim_ref[0:span, :] = ap[0]
    rim_ref[span : 2 * span, :] = ap[frames + 1]
    rim_ref[2 * span :, :] = stacked(loss, LOSS).astype(BF)


def temporal_forward(scale, odd, act, one, two, weight, clean, noise, token):
    frames, span, features = act.shape
    whole = lambda i: (0, 0, 0)
    head = pl.BlockSpec((frames, span, features), whole)
    halo = pl.BlockSpec((1, span, features), whole)
    return pl.pallas_call(
        temporal_forward_kernel,
        grid=(1,),
        in_specs=[
            pl.BlockSpec(memory_space=pltpu.SMEM),
            pl.BlockSpec(memory_space=pltpu.SMEM),
            head,
            halo,
            halo,
            pl.BlockSpec(weight.shape, whole),
            head,
            head,
            pl.BlockSpec(memory_space=pl.ANY),
        ],
        out_specs=[
            head,
            halo,
            halo,
            pl.BlockSpec((1, features), lambda i: (0, 0)),
            pl.BlockSpec((2 * span + LOSS, features), lambda i: (0, 0)),
        ],
        out_shape=[
            jax.ShapeDtypeStruct((frames, span, features), BF),
            jax.ShapeDtypeStruct((1, span, features), BF),
            jax.ShapeDtypeStruct((1, span, features), BF),
            jax.ShapeDtypeStruct((1, features), F32),
            jax.ShapeDtypeStruct((2 * span + LOSS, features), BF),
        ],
        scratch_shapes=[pltpu.VMEM((frames + 2, span, features), BF)],
        compiler_params=params(16),
        cost_estimate=cost(2 * 3 * frames * span * features * features, 6 * features * features),
        name="temporal_forward",
    )(scale, odd, act, one, two, weight, clean, noise, token)


def thirds(value):
    high = value.astype(BF)
    rest = value - high.astype(F32)
    middle = rest.astype(BF)
    return high, middle, (rest - middle.astype(F32)).astype(BF)


def stacked(value, rows):
    high, middle, low = thirds(value)
    row = lax.broadcasted_iota(jnp.int32, (rows, value.shape[1]), 0)
    parts = [p.astype(F32) for p in (high, middle, low)]
    return jnp.where(
        row == 0, parts[0], jnp.where(row == 1, parts[1], jnp.where(row == 2, parts[2], 0.0))
    )


def joined(rows):
    return (rows[0:1] + rows[1:2]) + rows[2:3]


def temporal_grad_kernel(
    bits_ref,
    act_ref,
    rim_ref,
    act_other_ref,
    rim_other_ref,
    gp_ref,
    gp_other_ref,
    choice_ref,
    reorder_ref,
    loss_ref,
    send_ref,
    keep_0,
    keep_1,
    keep_2,
    sum_ref,
    padded,
    chosen,
    gps,
    total,
    choice,
    reorder,
    sems,
):
    frames, span, features = gp_ref.shape
    core = bits_ref[3]
    half = features // 2
    rows = half // 2
    lanes = loss_ref[...] + joined(rim_other_ref[2 * span : 2 * span + LOSS, :].astype(F32))
    lane = lax.broadcasted_iota(jnp.int32, lanes.shape, 1)
    loss = jnp.where(lane == bits_ref[4], jnp.sum(lanes, axis=1, keepdims=True), 0.0)
    sum_ref[...] = loss
    copies = [
        pltpu.make_async_copy(choice_ref.at[core], choice, sems.at[0]),
        pltpu.make_async_copy(reorder_ref.at[core], reorder, sems.at[1]),
    ]
    for c in copies:
        c.start()
    for which, (act, rim) in enumerate(((act_ref, rim_ref), (act_other_ref, rim_other_ref))):
        padded[which, 0] = rim[0:span, :]
        padded[which, 1 : frames + 1] = act[...]
        padded[which, frames + 1] = rim[span : 2 * span, :]
    for c in copies:
        c.wait()
    chosen[...] = lax.dot_general(
        choice[...],
        padded[...].reshape(-1, features),
        (((1,), (1,)), ((), ())),
        preferred_element_type=F32,
    ).astype(BF)
    gps[0:frames] = gp_ref[...]
    gps[frames:] = gp_other_ref[...]
    for tap, keep in enumerate((keep_0, keep_1, keep_2)):
        here = tap * span
        there = here + (frames + 2) * span
        long = frames * span
        left = jnp.concatenate(
            [chosen[:, here : here + long], chosen[:, there : there + long]], axis=1
        )
        if tap > 0:
            left = jnp.dot(
                reorder[tap - 1], left, preferred_element_type=F32
            ).astype(BF)
        total[...] = jnp.dot(
            left, gps[...].reshape(2 * long, features), preferred_element_type=F32
        )
        bit = bits_ref[tap]
        kept = pl.ds(pl.multiple_of(bit * rows, rows), rows)
        sent = pl.ds(pl.multiple_of((1 - bit) * rows, rows), rows)
        keep[...] = total[kept, :]
        send_ref[tap, 0:rows, :] = total[sent, :].astype(BF)
        send_ref[tap, rows : rows + LOSS, :] = stacked(loss, LOSS).astype(BF)
        send_ref[tap, rows + LOSS :, :] = jnp.zeros(
            (send_ref.shape[1] - rows - LOSS, features), BF
        )


def temporal_grad_local(
    bits, act, rim, act_other, rim_other, gp, gp_other, choice, reorder, loss
):
    frames, span, features = gp.shape
    rows = features // 4
    vmem = pl.BlockSpec(memory_space=pltpu.VMEM)
    return pl.pallas_call(
        temporal_grad_kernel,
        in_specs=[pl.BlockSpec(memory_space=pltpu.SMEM)]
        + [vmem] * 6
        + [pl.BlockSpec(memory_space=pltpu.HBM)] * 2
        + [vmem],
        out_shape=[
            pltpu.VMEM((3, 3 * EXTRA, features), BF),
            *[pltpu.HBM((rows, features), F32) for _ in range(3)],
            pltpu.VMEM((1, features), F32),
        ],
        out_specs=[vmem] * 5,
        scratch_shapes=[
            pltpu.VMEM((2, frames + 2, span, features), BF),
            pltpu.VMEM((features // 2, 2 * (frames + 2) * span), BF),
            pltpu.VMEM((2 * frames, span, features), BF),
            pltpu.VMEM((features // 2, features), F32),
            pltpu.VMEM(choice.shape[1:], BF),
            pltpu.VMEM(reorder.shape[1:], BF),
            pltpu.SemaphoreType.DMA((2,)),
        ],
        compiler_params=params(20),
        cost_estimate=cost(
            2 * 4 * frames * span * features * features, 6 * features * features
        ),
        name="temporal_grad",
    )(bits, act, rim, act_other, rim_other, gp, gp_other, in_hbm(choice), in_hbm(reorder), loss)


def temporal_backward_kernel(
    odd, gp_ref, one_ref, two_ref, w_ref, der_ref, token, out_ref, pad
):
    frames, span, features = gp_ref.shape
    pad[(1 - odd[0]) * (frames + 1)] = one_ref[0]
    pad[odd[0] * (frames + 1)] = two_ref[0]
    pad[1 : frames + 1] = gp_ref[...]
    total = jnp.zeros((frames * span, features), F32)
    for tap in range(3):
        total = total + lax.dot_general(
            pad[2 - tap : 2 - tap + frames].reshape(frames * span, features),
            w_ref[tap],
            (((1,), (1,)), ((), ())),
            preferred_element_type=F32,
        )
    der = der_ref[...].reshape(frames * span, features)
    out_ref[...] = (total * der).astype(BF).reshape(frames, span, features)


def temporal_backward(odd, gp, one, two, weight, der, token):
    frames, span, features = gp.shape
    return pl.pallas_call(
        temporal_backward_kernel,
        in_specs=[pl.BlockSpec(memory_space=pltpu.SMEM)]
        + [pl.BlockSpec(memory_space=pltpu.VMEM)] * 5
        + [pl.BlockSpec(memory_space=pl.ANY)],
        out_shape=pltpu.VMEM((frames, span, features), BF),
        scratch_shapes=[pltpu.VMEM((frames + 2, span, features), BF)],
        compiler_params=params(12),
        cost_estimate=cost(2 * 3 * frames * span * features * features, 6 * features * features),
        name="temporal_backward",
    )(odd, gp, one, two, weight, der, token)


def select_latent_kernel(core_ref, x_ref, choice_ref, token, own_ref, send_ref):
    core = core_ref[0]
    x = x_ref[...].reshape(-1, x_ref.shape[2])
    for out, which in ((send_ref, 1 - core), (own_ref, core)):
        out[...] = lax.dot_general(
            choice_ref[which], x, (((1,), (1,)), ((), ())), preferred_element_type=F32
        ).astype(BF)


def selected_latent(core, x, choice, token):
    frames, span, channels = x.shape
    shape = jax.ShapeDtypeStruct((channels // 2, frames * span), BF)
    vmem = pl.BlockSpec(memory_space=pltpu.VMEM)
    return pl.pallas_call(
        select_latent_kernel,
        in_specs=[
            pl.BlockSpec(memory_space=pltpu.SMEM),
            vmem,
            vmem,
            pl.BlockSpec(memory_space=pl.ANY),
        ],
        out_specs=[vmem, vmem],
        out_shape=[shape, shape],
        compiler_params=params(16),
        cost_estimate=cost(2 * frames * span * channels * channels, 4 * channels * channels),
        name="select_latent",
    )(core, x, choice, token)


def arrange_latent_kernel(
    core_ref, own_ref, other_ref, reorder_ref, token, out_hbm, out_ref, reorder, sem, sems
):
    core = core_ref[0]
    copy = pltpu.make_async_copy(reorder_ref.at[core], reorder, sem)
    copy.start()
    frames = 5
    span = own_ref.shape[1] // frames
    for f in range(frames):
        here = pl.multiple_of((2 * f + core) * span, span)
        there = pl.multiple_of((2 * f + 1 - core) * span, span)
        out_ref[0, :, pl.ds(here, span)] = own_ref[:, f * span : (f + 1) * span]
        out_ref[0, :, pl.ds(there, span)] = other_ref[:, f * span : (f + 1) * span]
    copy.wait()
    copies = [pltpu.make_async_copy(out_ref.at[k], out_hbm.at[k], sems.at[k]) for k in range(3)]
    copies[0].start()
    for third in range(1, 3):
        out_ref[third] = jnp.dot(
            reorder[third - 1], out_ref[0], preferred_element_type=F32
        ).astype(BF)
        copies[third].start()
    for c in copies:
        c.wait()


def arranged_latent(core, own, other, reorder, token):
    half, positions = own.shape
    vmem = pl.BlockSpec(memory_space=pltpu.VMEM)
    return pl.pallas_call(
        arrange_latent_kernel,
        in_specs=[
            pl.BlockSpec(memory_space=pltpu.SMEM),
            vmem,
            vmem,
            pl.BlockSpec(memory_space=pltpu.HBM),
            pl.BlockSpec(memory_space=pl.ANY),
        ],
        out_specs=pl.BlockSpec(memory_space=pltpu.HBM),
        out_shape=pltpu.HBM((3, half, 2 * positions), BF),
        scratch_shapes=[
            pltpu.VMEM((3, half, 2 * positions), BF),
            pltpu.VMEM(reorder.shape[1:], BF),
            pltpu.SemaphoreType.DMA,
            pltpu.SemaphoreType.DMA((3,)),
        ],
        compiler_params=params(16),
        cost_estimate=cost(8 * half * half * positions, 20 * half * positions),
        name="arrange_latent",
    )(core, own, other, in_hbm(reorder), token)


def shifted_gradient(core, own_ref, other_ref, pad):
    frames, span, features = own_ref.shape
    cols = (pad.shape[2] - 2 * span) // 2
    col = lax.broadcasted_iota(jnp.int32, (span, features), 0) % cols
    rim = jnp.zeros((cols, features), BF)

    def one(f, carry):
        for b in range(3):
            pad[b, f, 0:cols, :] = rim
            pad[b, f, cols + 2 * span : 2 * cols + 2 * span, :] = rim
        for ref, place in ((own_ref, core), (other_ref, 1 - core)):
            rows = pl.ds(pl.multiple_of(cols + place * span, cols), span)
            here = ref[f]
            wide = here.astype(F32)
            later = jnp.where(col == cols - 1, 0.0, pltpu.roll(wide, span - 1, 0))
            sooner = jnp.where(col == 0, 0.0, pltpu.roll(wide, 1, 0))
            pad[0, f, rows, :] = later.astype(BF)
            pad[1, f, rows, :] = here
            pad[2, f, rows, :] = sooner.astype(BF)
        return carry

    lax.fori_loop(0, frames, one, 0)


def gradient_send_kernel(thirds, where, lat_ref, own_ref, other_ref, extra_ref, *rest):
    outs, (pad, lat, lat_sems) = rest[: len(thirds)], rest[len(thirds) :]
    frames, span, features = own_ref.shape
    cols = pad.shape[2] // 2 - span
    height = lat.shape[1]
    copies = []
    for k, first in enumerate(thirds):
        rows = pl.ds(pl.multiple_of(where[1 + first] * height, height), height)
        copies.append(
            pltpu.make_async_copy(lat_ref.at[first, rows, :], lat.at[k], lat_sems.at[k])
        )
    for c in copies:
        c.start()
    shifted_gradient(where[0], own_ref, other_ref, pad)
    for k, first in enumerate(thirds):
        copies[k].wait()
        start = (2 - first) * cols
        for second in range(3):
            grad = pad[second, :, start : start + 2 * span, :]
            outs[k][second, 0:height, :] = jnp.dot(
                lat[k], grad.reshape(2 * frames * span, features), preferred_element_type=F32
            ).astype(BF)
            outs[k][second, height:, :] = extra_ref[first, second * EXTRA : (second + 1) * EXTRA, :]


def gradient_send(thirds, where, lat, own, other, extra, name):
    frames, span, features = own.shape
    rows = lat.shape[1] // 2
    cols = 16
    n = len(thirds)
    vmem = pl.BlockSpec(memory_space=pltpu.VMEM)
    hbm = pl.BlockSpec(memory_space=pltpu.HBM)
    return pl.pallas_call(
        functools.partial(gradient_send_kernel, thirds),
        in_specs=[pl.BlockSpec(memory_space=pltpu.SMEM), hbm] + [vmem] * 3,
        out_specs=[vmem] * n,
        out_shape=[pltpu.VMEM((3, rows + EXTRA, features), BF)] * n,
        scratch_shapes=[
            pltpu.VMEM((3, frames, 2 * span + 2 * cols, features), BF),
            pltpu.VMEM((n, rows, lat.shape[2]), BF),
            pltpu.SemaphoreType.DMA((n,)),
        ],
        compiler_params=params(28),
        cost_estimate=cost(1, 1),
        name=name,
    )(where, in_hbm(lat), own, other, in_vmem(extra))


def gradient_keep_kernel(where, lat_ref, own_ref, other_ref, out_ref, pad, lat, lat_sems, sums, sems):
    frames, span, features = own_ref.shape
    cols = pad.shape[2] // 2 - span
    height = lat.shape[1]
    copies = []
    for k in range(3):
        rows = pl.ds(pl.multiple_of(where[1 + k] * height, height), height)
        copies.append(pltpu.make_async_copy(lat_ref.at[k, rows, :], lat.at[k], lat_sems.at[k]))
    for c in copies:
        c.start()
    shifted_gradient(where[0], own_ref, other_ref, pad)
    for c in copies:
        c.wait()

    def one(k, carry):
        start = pl.multiple_of((2 - k) * cols, cols)
        for second in range(3):
            grad = pad[second, :, pl.ds(start, 2 * span), :]
            sums[k, second] = jnp.dot(
                lat[k], grad.reshape(2 * frames * span, features), preferred_element_type=F32
            )
        pltpu.make_async_copy(sums.at[k], out_ref.at[k], sems.at[k]).start()
        return carry

    lax.fori_loop(0, 3, one, 0)
    for k in range(3):
        pltpu.make_async_copy(sums.at[k], out_ref.at[k], sems.at[k]).wait()


def gradient_keep(where, lat, own, other):
    frames, span, features = own.shape
    rows = lat.shape[1] // 2
    cols = 16
    vmem = pl.BlockSpec(memory_space=pltpu.VMEM)
    hbm = pl.BlockSpec(memory_space=pltpu.HBM)
    return pl.pallas_call(
        gradient_keep_kernel,
        in_specs=[pl.BlockSpec(memory_space=pltpu.SMEM), hbm, vmem, vmem],
        out_specs=hbm,
        out_shape=pltpu.HBM((3, 3, rows, features), F32),
        scratch_shapes=[
            pltpu.VMEM((3, frames, 2 * span + 2 * cols, features), BF),
            pltpu.VMEM((3, rows, lat.shape[2]), BF),
            pltpu.SemaphoreType.DMA((3,)),
            pltpu.VMEM((3, 3, rows, features), F32),
            pltpu.SemaphoreType.DMA((3,)),
        ],
        compiler_params=params(28),
        cost_estimate=cost(1, 1),
        name="spatial_keep",
    )(where, in_hbm(lat), own, other)


def bit_of(value, kind):
    if kind == 0:
        return value // 2
    return (value + 1) // 2 % 2


def swap_pairs(axis, step, size):
    pairs = []
    stride = STRIDES[axis]
    for device in range(size):
        tm, core = divmod(device, 2)
        value = tm // stride % RING
        partner = (value ^ 1) if (step + core) % 2 == 0 else (RING - 1 - value)
        pairs.append((device, (tm + (partner - value) * stride) * 2 + core))
    return pairs


def owners(order, core):
    found = []
    for n in range(RING**3):
        place = 0
        for k, axis in enumerate(order):
            digit = n // RING ** (2 - k) % RING
            first, second = divmod(digit, 2)
            low, high = (second, first) if core == 0 else (first, second)
            value = 2 * low + (low ^ high)
            place += value * STRIDES[axis]
        found.append(2 * place + core)
    return np.array(found)


def one_hot(rows, width):
    return (rows[:, None] == np.arange(width)[None, :]).astype(np.float32)


def selections(channels):
    each = channels // (2 * RING**3)
    return np.stack(
        [
            one_hot((owners(ORDERS[0], c)[:, None] * each + np.arange(each)).reshape(-1), channels)
            for c in range(2)
        ]
    )


def reorders(channels):
    each = channels // (2 * RING**3)
    found = []
    for c in range(2):
        base = list(owners(ORDERS[0], c))
        for order in ORDERS[1:]:
            at = np.array([base.index(o) for o in owners(order, c)])
            rows = (at[:, None] * each + np.arange(each)).reshape(-1)
            found.append(one_hot(rows, channels // 2))
    return np.stack(found).reshape(2, 2, channels // 2, channels // 2)


def up_to(n, multiple):
    return -(-n // multiple) * multiple


def payload_rows(rows, more, has_loss):
    return 3 * up_to(rows, 16) + (LOSS if has_loss else 0) + up_to(more, 16)


def places(rows, has_loss):
    slab = up_to(rows, 16)
    return [0, slab, 2 * slab], 3 * slab, 3 * slab + (LOSS if has_loss else 0)


def halve(ref, bit, count, send_ref, send_at):
    part = count // 2
    sent = up_to(part, 16)
    kept = up_to(part, 8)
    if part % 16 == 0:
        mine = ref[pl.ds(pl.multiple_of(bit * part, part), part), :]
        theirs = ref[pl.ds(pl.multiple_of((1 - bit) * part, part), part), :]
    else:
        whole = ref[...]
        tall = whole.shape[0]
        mine = pltpu.roll(whole, (tall - bit * part) % tall, 0)[:kept]
        theirs = pltpu.roll(whole, (tall - (1 - bit) * part) % tall, 0)[:sent]
    send_ref[send_at : send_at + sent, :] = theirs.astype(send_ref.dtype)
    return mine


def combine_first_kernel(third, has_loss, bits, keep_ref, met_ref, tp_ref, *refs):
    refs = list(refs)
    loss_ref = refs.pop(0) if has_loss else None
    send_ref, sp_out, tp_out = refs[:3]
    refs = refs[3:]
    loss_out = refs.pop(0) if has_loss else None
    keep_buf, region, extra_buf, tp_buf, sems = refs
    rows, features = keep_ref.shape[2:]
    count = rows // 2
    copies = [
        pltpu.make_async_copy(met_ref.at[:, pl.ds(rows, EXTRA), :], extra_buf, sems.at[0]),
        pltpu.make_async_copy(tp_ref, tp_buf, sems.at[1]),
    ]
    for k, bit in enumerate((1 - bits[1], bits[1])):
        at = pl.multiple_of(bit * count, count)
        part = pl.ds(at, count)
        copies += [
            pltpu.make_async_copy(
                keep_ref.at[third, :, part, :], keep_buf.at[k], sems.at[2 + 2 * k]
            ),
            pltpu.make_async_copy(met_ref.at[:, part, :], region.at[k], sems.at[3 + 2 * k]),
        ]
    for c in copies:
        c.start()
    for c in copies[:4]:
        c.wait()
    for b in range(3):
        total = keep_buf[0, b] + region[0, b].astype(F32)
        send_ref[b * count : (b + 1) * count, :] = total.astype(BF)
    tall = tp_buf.shape[0]
    extra = extra_buf[...].reshape(3 * EXTRA, features).astype(F32)
    tp_buf[...] += extra[:tall]
    behind = 3 * count
    if has_loss:
        loss = loss_ref[...] + joined(extra[tall : tall + LOSS])
        loss_out[...] = loss
        send_ref[behind : behind + LOSS, :] = stacked(loss, LOSS).astype(BF)
        behind += LOSS
    tp_out[...] = halve(tp_buf, bits[1], tall, send_ref, behind)
    for c in copies[4:]:
        c.wait()
    for b in range(3):
        sp_out[b] = keep_buf[1, b] + region[1, b].astype(F32)


def combine_first(third, bits, keep, met, tp, loss, name):
    has_loss = loss is not None
    rows, width = keep.shape[2:]
    half = rows // 2
    vmem = pl.BlockSpec(memory_space=pltpu.VMEM)
    hbm = pl.BlockSpec(memory_space=pltpu.HBM)
    out_shape = [
        pltpu.VMEM((payload_rows(half, half // 2, has_loss), width), BF),
        pltpu.VMEM((3, half, width), F32),
        pltpu.VMEM((half // 2, width), F32),
    ]
    if has_loss:
        out_shape.append(pltpu.VMEM((1, width), F32))
    done = pl.pallas_call(
        functools.partial(combine_first_kernel, third, has_loss),
        in_specs=[pl.BlockSpec(memory_space=pltpu.SMEM), hbm, hbm, hbm] + [vmem] * has_loss,
        out_specs=[vmem] * len(out_shape),
        out_shape=out_shape,
        scratch_shapes=[
            pltpu.VMEM((2, 3, half, width), F32),
            pltpu.VMEM((2, 3, half, width), BF),
            pltpu.VMEM((3, EXTRA, width), BF),
            pltpu.VMEM((half, width), F32),
            pltpu.SemaphoreType.DMA((6,)),
        ],
        compiler_params=params(16),
        cost_estimate=cost(0, 8 * rows * width),
        name=name,
    )(bits, in_hbm(keep), in_hbm(met), in_hbm(tp), *([in_vmem(loss)] if has_loss else []))
    return done if has_loss else (*done, None)


def combine_kernel(rows, more, has_loss, bit_ref, met_ref, sp_ref, tp_ref, *rest):
    if has_loss:
        loss_ref, send_ref, sp_out, tp_out, loss_out, full, full_more = rest
    else:
        send_ref, sp_out, tp_out, full, full_more = rest
    bit = bit_ref[0]
    slabs, loss_at, behind = places(rows, has_loss)
    next_slab = up_to(rows // 2, 16)
    for b in range(3):
        tall = full.shape[1]
        full[b] = sp_ref[b] + met_ref[slabs[b] : slabs[b] + tall, :].astype(F32)
        sp_out[b] = halve(full.at[b], bit, rows, send_ref, b * next_slab)
    tall = full_more.shape[0]
    full_more[...] = tp_ref[...] + met_ref[behind : behind + tall, :].astype(F32)
    behind = 3 * next_slab
    if has_loss:
        loss = loss_ref[...] + joined(met_ref[loss_at : loss_at + LOSS, :].astype(F32))
        loss_out[...] = loss
        send_ref[behind : behind + LOSS, :] = stacked(loss, LOSS).astype(send_ref.dtype)
        behind += LOSS
    tp_out[...] = halve(full_more, bit, more, send_ref, behind)


def combine(bit, met, sp, tp, loss, rows, more, name):
    has_loss = loss is not None
    width = met.shape[1]
    out_shape = [
        pltpu.VMEM((payload_rows(rows // 2, more // 2, has_loss), width), BF),
        pltpu.VMEM((3, up_to(rows // 2, 8), width), F32),
        pltpu.VMEM((up_to(more // 2, 8), width), F32),
    ]
    operands = [bit, in_vmem(met), in_vmem(sp), in_vmem(tp)]
    if has_loss:
        out_shape.append(pltpu.VMEM((1, width), F32))
        operands.append(in_vmem(loss))
    vmem = pl.BlockSpec(memory_space=pltpu.VMEM)
    done = pl.pallas_call(
        functools.partial(combine_kernel, rows, more, has_loss),
        in_specs=[pl.BlockSpec(memory_space=pltpu.SMEM)] + [vmem] * (len(operands) - 1),
        out_specs=[vmem] * len(out_shape),
        out_shape=out_shape,
        scratch_shapes=[pltpu.VMEM(sp.shape, F32), pltpu.VMEM(tp.shape, F32)],
        compiler_params=params(12),
        cost_estimate=cost(0, 8 * sp.size),
        name=name,
    )(*operands)
    return done if has_loss else (*done, None)


def on_device(clean, noise, timestep, spatial_weight, temporal_weight):
    frames, rows, cols, channels = clean.shape
    features = temporal_weight.shape[0]
    span = rows * cols
    blocks = lax.axis_size("tm")
    size = 2 * blocks
    tm = lax.axis_index("tm")
    core = lax.axis_index("space")
    both = ("tm", "space")
    step_value = timestep[0].astype(F32)
    angle = math.pi / 2.0 * (step_value + 1.0) / (STEPS + 1.0)
    signal = jnp.cos(angle)
    sigma = jnp.sin(angle)
    positions = frames * blocks * rows * 2 * cols
    scale = jnp.stack([signal, sigma, jnp.float32(math.sqrt(positions))])
    w_spatial = jnp.transpose(spatial_weight, (1, 2, 0, 3))
    w_temporal = jnp.transpose(temporal_weight, (1, 0, 2))

    def mix(c, n):
        return (signal * c.astype(F32) + sigma * n.astype(F32)).astype(BF)

    edge_at = (1 - core) * (rows - 1)
    edge = mix(
        lax.dynamic_slice_in_dim(clean, edge_at, 1, axis=1),
        lax.dynamic_slice_in_dim(noise, edge_at, 1, axis=1),
    )
    met = lax.ppermute(edge, "space", [(0, 1), (1, 0)]).reshape(frames, cols, channels)
    above = jnp.where(core == 0, jnp.zeros_like(met), met)
    below = jnp.where(core == 0, met, jnp.zeros_like(met))
    noisy = mix(clean, noise).reshape(frames, span, channels)
    cross = [(0, 1), (1, 0)]
    core_index = jnp.reshape(core, (1,)).astype(jnp.int32)
    odd = jnp.reshape(tm % 2, (1,)).astype(jnp.int32)
    act, act_one, act_two, der = spatial_forward(odd, noisy, above, below, w_spatial)

    per_clip = CLIP // frames
    shift = CLIP // 4 // frames
    swaps = []
    for low in range(2):
        pairs = [(i, i + 1) for i in range(low, blocks - 1, 2) if (i + 1 + shift) % per_clip != 0]
        swaps.append(pairs + [(j, i) for i, j in pairs])
    act_one = lax.ppermute(act_one, "tm", swaps[0])
    act_two = lax.ppermute(act_two, "tm", swaps[1])
    act_other = lax.ppermute(act, "space", cross)
    lat_own, lat_send = selected_latent(
        core_index, noisy, jnp.asarray(selections(channels), BF), der
    )
    lat_other = lax.ppermute(lat_send, "space", cross)
    flat = (frames, span, channels)
    gp, gp_one, gp_two, loss_lanes, rim = temporal_forward(
        scale,
        odd,
        act,
        act_one,
        act_two,
        w_temporal,
        clean.reshape(flat),
        noise.reshape(flat),
        lat_own,
    )
    gp_one = lax.ppermute(gp_one, "tm", swaps[0])
    gp_two = lax.ppermute(gp_two, "tm", swaps[1])
    gp_other = lax.ppermute(gp, "space", cross)
    rim_other = lax.ppermute(rim, "space", cross)
    bits = []
    for order in ORDERS:
        own = []
        for axis in order:
            value = tm // STRIDES[axis] % RING
            low, high = bit_of(value, 0), bit_of(value, 1)
            own.append(jnp.where(core == 0, high, low))
            own.append(jnp.where(core == 0, low, high))
        bits.append([b.astype(jnp.int32) for b in own])
    first_bits = jnp.stack([b[0] for b in bits])
    extra, *more_keeps, loss = temporal_grad_local(
        jnp.concatenate([first_bits, core_index, jnp.reshape(tm, (1,)).astype(jnp.int32)]),
        act,
        rim,
        act_other,
        rim_other,
        gp,
        gp_other,
        jnp.asarray(selections(features), BF),
        jnp.asarray(reorders(features), BF),
        loss_lanes,
    )
    gh = temporal_backward(odd, gp, gp_one, gp_two, w_temporal, der, loss)
    gh_other = lax.ppermute(gh, "space", cross)
    lat = arranged_latent(
        core_index, lat_own, lat_other, jnp.asarray(reorders(channels), BF), gh
    )
    send_at = jnp.concatenate([core_index, 1 - first_bits])
    keep_at = jnp.concatenate([core_index, first_bits])
    (send_1,) = gradient_send((1,), send_at, lat, gh, gh_other, extra, "spatial_send_first")
    send_2, send_0 = gradient_send((2, 0), send_at, lat, gh, gh_other, extra, "spatial_send_rest")
    sends = [send_0, send_1, send_2]
    keeps = gradient_keep(keep_at, lat, gh, gh_other)

    state = [
        (sends[t].reshape(-1, features), None, more_keeps[t], loss if t == 0 else None)
        for t in range(3)
    ]
    count, more = channels // 4, features // 4
    for step in range(6):
        met = [
            lax.ppermute(state[t][0], both, swap_pairs(ORDERS[t][step // 2], step, size))
            for t in range(3)
        ]
        if step == 5:
            break
        for t in range(3):
            _, sp, tp, total = state[t]
            name = "combine_%d_%d" % (step, t)
            if step == 0:
                arrived = met[t].reshape(sends[t].shape)
                state[t] = combine_first(t, jnp.stack(bits[t]), keeps, arrived, tp, total, name)
            else:
                bit = jnp.reshape(bits[t][step + 1], (1,))
                state[t] = combine(bit, met[t], sp, tp, total, count, more, name)
        count, more = count // 2, more // 2

    spatial_parts, temporal_parts = [], []
    for t in range(3):
        _, sp, tp, total = state[t]
        slabs, loss_at, behind = places(count, total is not None)
        spatial_parts.append(
            jnp.stack(
                [sp[b, :count] + met[t][s : s + count].astype(F32) for b, s in enumerate(slabs)]
            )
        )
        temporal_parts.append(tp[:more] + met[t][behind : behind + more].astype(F32))
        if total is not None:
            loss_sum = jnp.sum(total + joined(met[t][loss_at : loss_at + LOSS].astype(F32)))
    spatial_grad = jnp.transpose(jnp.stack(spatial_parts), (2, 0, 1, 3))
    temporal_grad = jnp.transpose(jnp.stack(temporal_parts), (1, 0, 2))
    return (loss_sum / (positions * features), spatial_grad, temporal_grad)


def solution(mesh):
    placed = (P("tm", "space", None, None), P("tm", "space", None, None), P(), P(), P())
    return jax.shard_map(
        on_device,
        mesh=mesh,
        in_specs=placed,
        out_specs=(P(), P(("tm", "space"), None, None, None), P(("tm", "space"), None, None)),
        check_vma=False,
    )
```

profile of v0, /device:TPU:0, one launch (start us, length us, event | category | flops | bytes accessed | tf_op | source)
XLA Modules:
  0.0 162.4 jit_solution(17080493232940969084)
XLA Ops:
  5.3 15.8 %spatial_forward.1 = (bf16[5,128,640]{2,1,0:T(8,128)(2,1)}, bf16[1,128,640]{2,1,0:T(8,128)(2,1)S(1)}, bf16[1,128,640]{2,1,0:T(8,128)(2,1)S(1)}, f32[5,128,640]{2,1,0:T(8,128)S(1)}) custom-call(s32[1]{0:T(128)} %bitcast.10.odd, bf16[5,128,1280]{2,1,0:T(8,128)(2,1)S(1)} %bitcast.104, bf16[5,16,1280]{2,1,0:T(8,128)(2,1)S(1)} %get-tuple-element.152.above_ref, ...), custom_call_target="tpu_custom_call" | custom-call | flops 9437184000 | bytes 14745600 | tf_op jit(solution)/shard_map/spatial_forward/pallas_call | solution.py:96
  25.7 2.7 %select_latent.1 = (bf16[640,640]{1,0:T(8,128)(2,1)S(1)}, bf16[640,640]{1,0:T(8,128)(2,1)S(1)}) custom-call(s32[1]{0:T(128)} %bitcast.6.core_ref, bf16[5,128,1280]{2,1,0:T(8,128)(2,1)S(1)} %bitcast.105, bf16[2,640,1280]{2,1,0:T(8,128)(2,1)S(1)} %copy-done.15, f32[5,128,640]{2,1,0:T(8,128)S(1)} %get-tuple-element.71.token.der_ref), custom_call_target="tpu_custom_call" | custom-call | flops 2097152000 | bytes 6553600 | tf_op jit(solution)/shard_map/select_latent/pallas_call | solution.py:380
  28.5 4.9 %temporal_forward.1 = (bf16[5,128,640]{2,1,0:T(8,128)(2,1)S(1)}, bf16[1,128,640]{2,1,0:T(8,128)(2,1)S(1)}, bf16[1,128,640]{2,1,0:T(8,128)(2,1)S(1)}, f32[1,640]{1,0:T(1,128)S(1)}, bf16[272,640]{1,0:T(8,128)(2,1)}) custom-call(f32[3]{0:T(128)S(1)} %pad_maximum_fusion.scale, s32[1]{0:T(128)} %bitcast.10.odd, bf16[5,128,640]{2,1,0:T(8,128)(2,1)} %get-tuple-element.74.act_ref, ...), custom_call_target="tpu_custom_call" | custom-call | flops 1572864000 | bytes 2457600 | tf_op jit(solution)/shard_map/temporal_forward/pallas_call | solution.py:166
  34.7 4.7 %collective-permute-start.4 = (bf16[1,128,640]{2,1,0:T(8,128)(2,1)}, bf16[1,128,640]{2,1,0:T(8,128)(2,1)S(1)}, u32[]{:S(2)}, u32[]{:S(2)}) collective-permute-start(bf16[1,128,640]{2,1,0:T(8,128)(2,1)} %copy-done.14), channel_id=1, source_target_pairs={{0,2},{4,6},{8,10},{12,14},{16,18},{20,22},{24,26},{28,30},{32,34}... | collective-permute-start | bytes 491528 | tf_op jit(solution)/shard_map/ppermute | solution.py:844
  40.2 8.0 %temporal_grad.1 = (bf16[3,192,640]{2,1,0:T(8,128)(2,1)S(1)}, f32[160,640]{1,0:T(8,128)}, f32[160,640]{1,0:T(8,128)}, f32[160,640]{1,0:T(8,128)}, f32[1,640]{1,0:T(1,128)S(1)}) custom-call(s32[5]{0:T(128)S(1)} %concatenate.12.bits_ref, bf16[5,128,640]{2,1,0:T(8,128)(2,1)} %get-tuple-element.74.act_ref, bf16[272,640]{1,0:T(8,128)(2,1)} %get-tuple-element.80.rim_ref, ...), custom_call_target="tpu_custom_call" | custom-call | flops 2097152000 | bytes 2457600 | tf_op jit(solution)/shard_map/temporal_grad/pallas_call | solution.py:304
  52.1 5.7 %arrange_latent.1.lat_ref = bf16[3,640,1280]{2,1,0:T(8,128)(2,1)} custom-call(s32[1]{0:T(128)} %bitcast.6.core_ref, bf16[640,640]{1,0:T(8,128)(2,1)S(1)} %copy-done.4, bf16[640,640]{1,0:T(8,128)(2,1)S(1)} %collective-permute-done.1.other_ref, bf16[2,2,640,640]{3,2,1,0:T(8,128)(2,1)} %constant.219.clone.reorder_ref, ...), custom_call_target="tpu_custom_call" | custom-call | flops 2097152000 | bytes 8192000 | tf_op jit(solution)/shard_map/arrange_latent/pallas_call | solution.py:424
  57.9 3.8 %spatial_send_first.1 = bf16[3,384,640]{2,1,0:T(8,128)(2,1)S(1)} custom-call(s32[4]{0:T(128)S(1)} %pad_add_fusion.1.where, bf16[3,640,1280]{2,1,0:T(8,128)(2,1)} %arrange_latent.1.lat_ref, bf16[5,128,640]{2,1,0:T(8,128)(2,1)S(1)} %temporal_backward.1.token.own_ref, bf16[5,128,640]{2,1,0:T(8,128)(2,1)S(1)} %collective-permute-done.9.other_ref, ...), custom_call_target="tpu_custom_call" | custom-call | flops 1 | bytes 1 | tf_op jit(solution)/shard_map/spatial_send_first/pallas_call | solution.py:503
  61.8 7.8 %collective-permute-start.16 = (bf16[1152,640]{1,0:T(8,128)(2,1)S(1)}, bf16[1152,640]{1,0:T(8,128)(2,1)}, u32[]{:S(2)}, u32[]{:S(2)}) collective-permute-start(bf16[1152,640]{1,0:T(8,128)(2,1)S(1)} %bitcast.106), channel_id=1, source_target_pairs={{0,8},{1,25},{2,10},{3,27},{4,12},{5,29},{6,14},{7,31},{8,0},{9,17... | collective-permute-start | bytes 4423688 | tf_op jit(solution)/shard_map/ppermute | solution.py:889
  69.5 7.5 %spatial_send_rest.1 = (bf16[3,384,640]{2,1,0:T(8,128)(2,1)}, bf16[3,384,640]{2,1,0:T(8,128)(2,1)}) custom-call(s32[4]{0:T(128)S(1)} %pad_add_fusion.1.where, bf16[3,640,1280]{2,1,0:T(8,128)(2,1)} %arrange_latent.1.lat_ref, bf16[5,128,640]{2,1,0:T(8,128)(2,1)S(1)} %temporal_backward.1.token.own_ref, ...), custom_call_target="tpu_custom_call" | custom-call | flops 1 | bytes 1 | tf_op jit(solution)/shard_map/spatial_send_rest/pallas_call | solution.py:503
  77.1 4.7 %collective-permute-start.10 = (bf16[1152,640]{1,0:T(8,128)(2,1)}, bf16[1152,640]{1,0:T(8,128)(2,1)}, u32[]{:S(2)}, u32[]{:S(2)}) collective-permute-start(bf16[1152,640]{1,0:T(8,128)(2,1)} %bitcast.18), channel_id=1, source_target_pairs={{0,32},{1,97},{2,34},{3,99},{4,36},{5,101},{6,38},{7,103},{8,40},{... | collective-permute-start | bytes 4423688 | tf_op jit(solution)/shard_map/ppermute | solution.py:889
  81.9 10.0 %spatial_keep.1.keep_ref = f32[3,3,320,640]{3,2,1,0:T(8,128)} custom-call(s32[4]{0:T(128)S(1)} %pad_add_fusion.where, bf16[3,640,1280]{2,1,0:T(8,128)(2,1)} %arrange_latent.1.lat_ref, bf16[5,128,640]{2,1,0:T(8,128)(2,1)S(1)} %temporal_backward.1.token.own_ref, bf16[5,128,640]{2,1,0:T(8,128)(2,1)S(1)} %collective-permute-done.9.other_ref), custom_call_target="tpu_custom_call" | custom-call | flops 1 | bytes 1 | tf_op jit(solution)/shard_map/spatial_keep/pallas_call | solution.py:554
  91.9 3.8 %combine_0_1.1 = (bf16[560,640]{1,0:T(8,128)(2,1)}, f32[3,160,640]{2,1,0:T(8,128)S(1)}, f32[80,640]{1,0:T(8,128)S(1)}) custom-call(s32[6]{0:T(128)S(1)} %stack.112.bits, f32[3,3,320,640]{3,2,1,0:T(8,128)} %spatial_keep.1.keep_ref, bf16[3,384,640]{2,1,0:T(8,128)(2,1)} %bitcast.28.met_ref, f32[160,640]{1,0:T(8,128)} %get-tuple-element.105.tp_ref), custom_call_target="tpu_custom_call" | custom-call | bytes 1638400 | tf_op jit(solution)/shard_map/combine_0_1/pallas_call | solution.py:716
  96.8 3.7 %combine_0_2.1 = (bf16[560,640]{1,0:T(8,128)(2,1)}, f32[3,160,640]{2,1,0:T(8,128)S(1)}, f32[80,640]{1,0:T(8,128)S(1)}) custom-call(s32[6]{0:T(128)S(1)} %stack.118.bits, f32[3,3,320,640]{3,2,1,0:T(8,128)} %spatial_keep.1.keep_ref, bf16[3,384,640]{2,1,0:T(8,128)(2,1)} %bitcast.37.met_ref, f32[160,640]{1,0:T(8,128)} %get-tuple-element.121.tp_ref), custom_call_target="tpu_custom_call" | custom-call | bytes 1638400 | tf_op jit(solution)/shard_map/combine_0_2/pallas_call | solution.py:716
  103.3 3.0 %combine_0_0.1 = (bf16[576,640]{1,0:T(8,128)(2,1)S(1)}, f32[3,160,640]{2,1,0:T(8,128)S(1)}, f32[80,640]{1,0:T(8,128)S(1)}, f32[1,640]{1,0:T(1,128)S(1)}) custom-call(s32[6]{0:T(128)S(1)} %stack.104.bits, f32[3,3,320,640]{3,2,1,0:T(8,128)} %spatial_keep.1.keep_ref, bf16[3,384,640]{2,1,0:T(8,128)(2,1)} %bitcast.19.met_ref, ...), custom_call_target="tpu_custom_call" | custom-call | bytes 1638400 | tf_op jit(solution)/shard_map/combine_0_0/pallas_call | solution.py:716
  106.3 4.2 %collective-permute-start.11 = (bf16[576,640]{1,0:T(8,128)(2,1)S(1)}, bf16[576,640]{1,0:T(8,128)(2,1)S(1)}, u32[]{:S(2)}, u32[]{:S(2)}) collective-permute-start(bf16[576,640]{1,0:T(8,128)(2,1)S(1)} %get-tuple-element.86), channel_id=1, source_target_pairs={{0,96},{1,33},{2,98},{3,35},{4,100},{5,37},{6,102},{7,39},{8,104},... | collective-permute-start | bytes 2211848 | tf_op jit(solution)/shard_map/ppermute | solution.py:889
  110.9 3.5 %collective-permute-done.23.met_ref = bf16[560,640]{1,0:T(8,128)(2,1)} collective-permute-done((bf16[560,640]{1,0:T(8,128)(2,1)}, bf16[560,640]{1,0:T(8,128)(2,1)}, u32[]{:S(2)}, u32[]{:S(2)}) %collective-permute-start.23) | collective-permute-done | bytes 716832 | tf_op jit(solution)/shard_map/ppermute | solution.py:889
  115.8 8.2 %collective-permute-start.24 = (bf16[288,640]{1,0:T(8,128)(2,1)S(1)}, bf16[288,640]{1,0:T(8,128)(2,1)S(1)}, u32[]{:S(2)}, u32[]{:S(2)}) collective-permute-start(bf16[288,640]{1,0:T(8,128)(2,1)S(1)} %get-tuple-element.125), channel_id=1, source_target_pairs={{0,32},{1,97},{2,34},{3,99},{4,36},{5,101},{6,38},{7,103},{8,40},{... | collective-permute-start | bytes 1105928 | tf_op jit(solution)/shard_map/ppermute | solution.py:889
  126.8 2.7 %collective-permute-start.19 = (bf16[176,640]{1,0:T(8,128)(2,1)S(1)}, bf16[176,640]{1,0:T(8,128)(2,1)S(1)}, u32[]{:S(2)}, u32[]{:S(2)}) collective-permute-start(bf16[176,640]{1,0:T(8,128)(2,1)S(1)} %get-tuple-element.112), channel_id=1, source_target_pairs={{0,6},{1,3},{2,4},{3,1},{4,2},{5,7},{6,0},{7,5},{8,14},{9,11},{10,... | collective-permute-start | bytes 675848 | tf_op jit(solution)/shard_map/ppermute | solution.py:889
  130.1 3.5 %collective-permute-start.25 = (bf16[176,640]{1,0:T(8,128)(2,1)S(1)}, bf16[176,640]{1,0:T(8,128)(2,1)S(1)}, u32[]{:S(2)}, u32[]{:S(2)}) collective-permute-start(bf16[176,640]{1,0:T(8,128)(2,1)S(1)} %get-tuple-element.128), channel_id=1, source_target_pairs={{0,96},{1,33},{2,98},{3,35},{4,100},{5,37},{6,102},{7,39},{8,104},... | collective-permute-start | bytes 675848 | tf_op jit(solution)/shard_map/ppermute | solution.py:889
  135.7 2.6 %collective-permute-done.25.met_ref = bf16[176,640]{1,0:T(8,128)(2,1)S(1)} collective-permute-done((bf16[176,640]{1,0:T(8,128)(2,1)S(1)}, bf16[176,640]{1,0:T(8,128)(2,1)S(1)}, u32[]{:S(2)}, u32[]{:S(2)}) %collective-permute-start.25) | collective-permute-done | bytes 225312 | tf_op jit(solution)/shard_map/ppermute | solution.py:889
  138.4 4.3 %collective-permute-start.26 = (bf16[112,640]{1,0:T(8,128)(2,1)S(1)}, bf16[112,640]{1,0:T(8,128)(2,1)S(1)}, u32[]{:S(2)}, u32[]{:S(2)}) collective-permute-start(bf16[112,640]{1,0:T(8,128)(2,1)S(1)} %get-tuple-element.131), channel_id=1, source_target_pairs={{0,8},{1,25},{2,10},{3,27},{4,12},{5,29},{6,14},{7,31},{8,0},{9,17... | collective-permute-start | bytes 430088 | tf_op jit(solution)/shard_map/ppermute | solution.py:889
  142.8 2.7 %collective-permute-start.21 = (bf16[64,640]{1,0:T(8,128)(2,1)S(1)}, bf16[64,640]{1,0:T(8,128)(2,1)S(1)}, u32[]{:S(2)}, u32[]{:S(2)}) collective-permute-start(bf16[64,640]{1,0:T(8,128)(2,1)S(1)} %get-tuple-element.119), channel_id=1, source_target_pairs={{0,96},{1,33},{2,98},{3,35},{4,100},{5,37},{6,102},{7,39},{8,104},... | collective-permute-start | bytes 245768 | tf_op jit(solution)/shard_map/ppermute | solution.py:889
  148.5 3.8 %collective-permute-done.27 = bf16[64,640]{1,0:T(8,128)(2,1)S(1)} collective-permute-done((bf16[64,640]{1,0:T(8,128)(2,1)S(1)}, bf16[64,640]{1,0:T(8,128)(2,1)S(1)}, u32[]{:S(2)}, u32[]{:S(2)}) %collective-permute-start.27) | collective-permute-done | bytes 81952 | tf_op jit(solution)/shard_map/ppermute | solution.py:889
  153.3 5.1 %collective-permute-done.15 = bf16[80,640]{1,0:T(8,128)(2,1)S(1)} collective-permute-done((bf16[80,640]{1,0:T(8,128)(2,1)S(1)}, bf16[80,640]{1,0:T(8,128)(2,1)S(1)}, u32[]{:S(2)}, u32[]{:S(2)}) %collective-permute-start.15) | collective-permute-done | bytes 102432 | tf_op jit(solution)/shard_map/ppermute | solution.py:889
  (113 shorter events, 32.1 us)
Async XLA Ops:
  21.2 7.2 %collective-permute-start.2 = (bf16[1,128,640]{2,1,0:T(8,128)(2,1)S(1)}, bf16[1,128,640]{2,1,0:T(8,128)(2,1)S(1)}, u32[]{:S(2)}, u32[]{:S(2)}) collective-permute-start(bf16[1,128,640]{2,1,0:T(8,128)(2,1)S(1)} %get-tuple-element.75), channel_id=1, source_target_pairs={{0,2},{4,6},{8,10},{12,14},{16,18},{20,22},{24,26},{28,30},{32,34}... | collective-permute-start | bytes 491528 | tf_op jit(solution)/shard_map/ppermute | solution.py:825
  23.9 16.3 %collective-permute-start.6 = (bf16[5,128,640]{2,1,0:T(8,128)(2,1)}, bf16[5,128,640]{2,1,0:T(8,128)(2,1)}, u32[]{:S(2)}, u32[]{:S(2)}) collective-permute-start(bf16[5,128,640]{2,1,0:T(8,128)(2,1)} %get-tuple-element.74.act_ref), channel_id=1, source_target_pairs={{0,1},{1,0},{2,3},{3,2},{4,5},{5,4},{6,7},{7,6},{8,9},{9,8},{10,11... | collective-permute-start | bytes 2457608 | tf_op jit(solution)/shard_map/ppermute | solution.py:827
  33.4 6.8 %collective-permute-start.8 = (bf16[5,128,640]{2,1,0:T(8,128)(2,1)S(1)}, bf16[5,128,640]{2,1,0:T(8,128)(2,1)}, u32[]{:S(2)}, u32[]{:S(2)}) collective-permute-start(bf16[5,128,640]{2,1,0:T(8,128)(2,1)S(1)} %get-tuple-element.77.gp_ref), channel_id=1, source_target_pairs={{0,1},{1,0},{2,3},{3,2},{4,5},{5,4},{6,7},{7,6},{8,9},{9,8},{10,11... | collective-permute-start | bytes 2457608 | tf_op jit(solution)/shard_map/ppermute | solution.py:846
  34.5 17.7 %collective-permute-start.1 = (bf16[640,640]{1,0:T(8,128)(2,1)}, bf16[640,640]{1,0:T(8,128)(2,1)S(1)}, u32[]{:S(2)}, u32[]{:S(2)}) collective-permute-start(bf16[640,640]{1,0:T(8,128)(2,1)} %copy-done.13), channel_id=1, source_target_pairs={{0,1},{1,0},{2,3},{3,2},{4,5},{5,4},{6,7},{7,6},{8,9},{9,8},{10,11... | collective-permute-start | bytes 2457608 | tf_op jit(solution)/shard_map/ppermute | solution.py:831
  34.7 13.5 %collective-permute-start.4 = (bf16[1,128,640]{2,1,0:T(8,128)(2,1)}, bf16[1,128,640]{2,1,0:T(8,128)(2,1)S(1)}, u32[]{:S(2)}, u32[]{:S(2)}) collective-permute-start(bf16[1,128,640]{2,1,0:T(8,128)(2,1)} %copy-done.14), channel_id=1, source_target_pairs={{0,2},{4,6},{8,10},{12,14},{16,18},{20,22},{24,26},{28,30},{32,34}... | collective-permute-start | bytes 491528 | tf_op jit(solution)/shard_map/ppermute | solution.py:844
  39.3 8.9 %collective-permute-start.5 = (bf16[1,128,640]{2,1,0:T(8,128)(2,1)S(1)}, bf16[1,128,640]{2,1,0:T(8,128)(2,1)S(1)}, u32[]{:S(2)}, u32[]{:S(2)}) collective-permute-start(bf16[1,128,640]{2,1,0:T(8,128)(2,1)S(1)} %get-tuple-element.79), channel_id=1, source_target_pairs={{2,4},{6,8},{10,12},{14,16},{18,20},{26,28},{30,32},{34,36},{38,40... | collective-permute-start | bytes 491528 | tf_op jit(solution)/shard_map/ppermute | solution.py:845
  51.8 6.1 %collective-permute-start.9 = (bf16[5,128,640]{2,1,0:T(8,128)(2,1)S(1)}, bf16[5,128,640]{2,1,0:T(8,128)(2,1)S(1)}, u32[]{:S(2)}, u32[]{:S(2)}) collective-permute-start(bf16[5,128,640]{2,1,0:T(8,128)(2,1)S(1)} %temporal_backward.1.token.own_ref), channel_id=1, source_target_pairs={{0,1},{1,0},{2,3},{3,2},{4,5},{5,4},{6,7},{7,6},{8,9},{9,8},{10,11... | collective-permute-start | bytes 2457608 | tf_op jit(solution)/shard_map/ppermute | solution.py:871
  61.8 30.2 %collective-permute-start.16 = (bf16[1152,640]{1,0:T(8,128)(2,1)S(1)}, bf16[1152,640]{1,0:T(8,128)(2,1)}, u32[]{:S(2)}, u32[]{:S(2)}) collective-permute-start(bf16[1152,640]{1,0:T(8,128)(2,1)S(1)} %bitcast.106), channel_id=1, source_target_pairs={{0,8},{1,25},{2,10},{3,27},{4,12},{5,29},{6,14},{7,31},{8,0},{9,17... | collective-permute-start | bytes 4423688 | tf_op jit(solution)/shard_map/ppermute | solution.py:889
  77.0 19.8 %collective-permute-start.22 = (bf16[1152,640]{1,0:T(8,128)(2,1)}, bf16[1152,640]{1,0:T(8,128)(2,1)}, u32[]{:S(2)}, u32[]{:S(2)}) collective-permute-start(bf16[1152,640]{1,0:T(8,128)(2,1)} %bitcast.36), channel_id=1, source_target_pairs={{0,2},{1,7},{2,0},{3,5},{4,6},{5,3},{6,4},{7,1},{8,10},{9,15},{10,... | collective-permute-start | bytes 4423688 | tf_op jit(solution)/shard_map/ppermute | solution.py:889
  77.1 26.2 %collective-permute-start.10 = (bf16[1152,640]{1,0:T(8,128)(2,1)}, bf16[1152,640]{1,0:T(8,128)(2,1)}, u32[]{:S(2)}, u32[]{:S(2)}) collective-permute-start(bf16[1152,640]{1,0:T(8,128)(2,1)} %bitcast.18), channel_id=1, source_target_pairs={{0,32},{1,97},{2,34},{3,99},{4,36},{5,101},{6,38},{7,103},{8,40},{... | collective-permute-start | bytes 4423688 | tf_op jit(solution)/shard_map/ppermute | solution.py:889
  95.7 14.8 %collective-permute-start.17 = (bf16[560,640]{1,0:T(8,128)(2,1)}, bf16[560,640]{1,0:T(8,128)(2,1)S(1)}, u32[]{:S(2)}, u32[]{:S(2)}) collective-permute-start(bf16[560,640]{1,0:T(8,128)(2,1)} %get-tuple-element.106), channel_id=1, source_target_pairs={{0,24},{1,9},{2,26},{3,11},{4,28},{5,13},{6,30},{7,15},{8,16},{9,1... | collective-permute-start | bytes 2150408 | tf_op jit(solution)/shard_map/ppermute | solution.py:889
  101.2 13.2 %collective-permute-start.23 = (bf16[560,640]{1,0:T(8,128)(2,1)}, bf16[560,640]{1,0:T(8,128)(2,1)}, u32[]{:S(2)}, u32[]{:S(2)}) collective-permute-start(bf16[560,640]{1,0:T(8,128)(2,1)} %get-tuple-element.122), channel_id=1, source_target_pairs={{0,6},{1,3},{2,4},{3,1},{4,2},{5,7},{6,0},{7,5},{8,14},{9,11},{10,... | collective-permute-start | bytes 2150408 | tf_op jit(solution)/shard_map/ppermute | solution.py:889
  106.3 17.7 %collective-permute-start.11 = (bf16[576,640]{1,0:T(8,128)(2,1)S(1)}, bf16[576,640]{1,0:T(8,128)(2,1)S(1)}, u32[]{:S(2)}, u32[]{:S(2)}) collective-permute-start(bf16[576,640]{1,0:T(8,128)(2,1)S(1)} %get-tuple-element.86), channel_id=1, source_target_pairs={{0,96},{1,33},{2,98},{3,35},{4,100},{5,37},{6,102},{7,39},{8,104},... | collective-permute-start | bytes 2211848 | tf_op jit(solution)/shard_map/ppermute | solution.py:889
  110.8 15.6 %collective-permute-start.18 = (bf16[288,640]{1,0:T(8,128)(2,1)S(1)}, bf16[288,640]{1,0:T(8,128)(2,1)S(1)}, u32[]{:S(2)}, u32[]{:S(2)}) collective-permute-start(bf16[288,640]{1,0:T(8,128)(2,1)S(1)} %get-tuple-element.109), channel_id=1, source_target_pairs={{0,2},{1,7},{2,0},{3,5},{4,6},{5,3},{6,4},{7,1},{8,10},{9,15},{10,... | collective-permute-start | bytes 1105928 | tf_op jit(solution)/shard_map/ppermute | solution.py:889
  115.8 13.9 %collective-permute-start.24 = (bf16[288,640]{1,0:T(8,128)(2,1)S(1)}, bf16[288,640]{1,0:T(8,128)(2,1)S(1)}, u32[]{:S(2)}, u32[]{:S(2)}) collective-permute-start(bf16[288,640]{1,0:T(8,128)(2,1)S(1)} %get-tuple-element.125), channel_id=1, source_target_pairs={{0,32},{1,97},{2,34},{3,99},{4,36},{5,101},{6,38},{7,103},{8,40},{... | collective-permute-start | bytes 1105928 | tf_op jit(solution)/shard_map/ppermute | solution.py:889
  124.3 9.3 %collective-permute-start.12 = (bf16[304,640]{1,0:T(8,128)(2,1)S(1)}, bf16[304,640]{1,0:T(8,128)(2,1)S(1)}, u32[]{:S(2)}, u32[]{:S(2)}) collective-permute-start(bf16[304,640]{1,0:T(8,128)(2,1)S(1)} %get-tuple-element.90), channel_id=1, source_target_pairs={{0,8},{1,25},{2,10},{3,27},{4,12},{5,29},{6,14},{7,31},{8,0},{9,17... | collective-permute-start | bytes 1167368 | tf_op jit(solution)/shard_map/ppermute | solution.py:889
  126.8 7.3 %collective-permute-start.19 = (bf16[176,640]{1,0:T(8,128)(2,1)S(1)}, bf16[176,640]{1,0:T(8,128)(2,1)S(1)}, u32[]{:S(2)}, u32[]{:S(2)}) collective-permute-start(bf16[176,640]{1,0:T(8,128)(2,1)S(1)} %get-tuple-element.112), channel_id=1, source_target_pairs={{0,6},{1,3},{2,4},{3,1},{4,2},{5,7},{6,0},{7,5},{8,14},{9,11},{10,... | collective-permute-start | bytes 675848 | tf_op jit(solution)/shard_map/ppermute | solution.py:889
  130.1 8.2 %collective-permute-start.25 = (bf16[176,640]{1,0:T(8,128)(2,1)S(1)}, bf16[176,640]{1,0:T(8,128)(2,1)S(1)}, u32[]{:S(2)}, u32[]{:S(2)}) collective-permute-start(bf16[176,640]{1,0:T(8,128)(2,1)S(1)} %get-tuple-element.128), channel_id=1, source_target_pairs={{0,96},{1,33},{2,98},{3,35},{4,100},{5,37},{6,102},{7,39},{8,104},... | collective-permute-start | bytes 675848 | tf_op jit(solution)/shard_map/ppermute | solution.py:889
  134.0 11.5 %collective-permute-start.13 = (bf16[192,640]{1,0:T(8,128)(2,1)S(1)}, bf16[192,640]{1,0:T(8,128)(2,1)S(1)}, u32[]{:S(2)}, u32[]{:S(2)}) collective-permute-start(bf16[192,640]{1,0:T(8,128)(2,1)S(1)} %get-tuple-element.94), channel_id=1, source_target_pairs={{0,24},{1,9},{2,26},{3,11},{4,28},{5,13},{6,30},{7,15},{8,16},{9,1... | collective-permute-start | bytes 737288 | tf_op jit(solution)/shard_map/ppermute | solution.py:889
  134.2 8.5 %collective-permute-start.20 = (bf16[112,640]{1,0:T(8,128)(2,1)S(1)}, bf16[112,640]{1,0:T(8,128)(2,1)S(1)}, u32[]{:S(2)}, u32[]{:S(2)}) collective-permute-start(bf16[112,640]{1,0:T(8,128)(2,1)S(1)} %get-tuple-element.115), channel_id=1, source_target_pairs={{0,32},{1,97},{2,34},{3,99},{4,36},{5,101},{6,38},{7,103},{8,40},{... | collective-permute-start | bytes 430088 | tf_op jit(solution)/shard_map/ppermute | solution.py:889
  138.4 8.1 %collective-permute-start.26 = (bf16[112,640]{1,0:T(8,128)(2,1)S(1)}, bf16[112,640]{1,0:T(8,128)(2,1)S(1)}, u32[]{:S(2)}, u32[]{:S(2)}) collective-permute-start(bf16[112,640]{1,0:T(8,128)(2,1)S(1)} %get-tuple-element.131), channel_id=1, source_target_pairs={{0,8},{1,25},{2,10},{3,27},{4,12},{5,29},{6,14},{7,31},{8,0},{9,17... | collective-permute-start | bytes 430088 | tf_op jit(solution)/shard_map/ppermute | solution.py:889
  142.8 5.7 %collective-permute-start.21 = (bf16[64,640]{1,0:T(8,128)(2,1)S(1)}, bf16[64,640]{1,0:T(8,128)(2,1)S(1)}, u32[]{:S(2)}, u32[]{:S(2)}) collective-permute-start(bf16[64,640]{1,0:T(8,128)(2,1)S(1)} %get-tuple-element.119), channel_id=1, source_target_pairs={{0,96},{1,33},{2,98},{3,35},{4,100},{5,37},{6,102},{7,39},{8,104},... | collective-permute-start | bytes 245768 | tf_op jit(solution)/shard_map/ppermute | solution.py:889
  145.7 6.7 %collective-permute-start.14 = (bf16[128,640]{1,0:T(8,128)(2,1)S(1)}, bf16[128,640]{1,0:T(8,128)(2,1)S(1)}, u32[]{:S(2)}, u32[]{:S(2)}) collective-permute-start(bf16[128,640]{1,0:T(8,128)(2,1)S(1)} %get-tuple-element.98), channel_id=1, source_target_pairs={{0,2},{1,7},{2,0},{3,5},{4,6},{5,3},{6,4},{7,1},{8,10},{9,15},{10,... | collective-permute-start | bytes 491528 | tf_op jit(solution)/shard_map/ppermute | solution.py:889
  152.5 6.0 %collective-permute-start.15 = (bf16[80,640]{1,0:T(8,128)(2,1)S(1)}, bf16[80,640]{1,0:T(8,128)(2,1)S(1)}, u32[]{:S(2)}, u32[]{:S(2)}) collective-permute-start(bf16[80,640]{1,0:T(8,128)(2,1)S(1)} %get-tuple-element.103), channel_id=1, source_target_pairs={{0,6},{1,3},{2,4},{3,1},{4,2},{5,7},{6,0},{7,5},{8,14},{9,11},{10,... | collective-permute-start | bytes 307208 | tf_op jit(solution)/shard_map/ppermute | solution.py:889
  (20 other events, 117.0 us)
where the time goes:
time: 163 us; the launch traced here: 162 us
  Pallas kernels  75.1 us (46%)
  starting transfers between devices  54.8 us (34%)
  waiting for transfers between devices  18.6 us (11%)
  local copies, waits for them, and re-layouts  5.39 us (3%)
  other arithmetic  4.73 us (3%)
  between operations  3.72 us (2%)
    ppermute x18, starting transfers between devices, on_device(): lax.ppermute(state[t][0], both, swap_pairs(ORDERS[t][step // 2], step, si...  45 us
    ppermute x18, waiting for transfers between devices, on_device(): lax.ppermute(state[t][0], both, swap_pairs(ORDERS[t][step // 2], step, si...  18.6 us
    pallas_call x1, Pallas kernels, spatial_forward(): pl.pallas_call(spatial_forward_kernel, grid=(3,), in_specs=[pl.BlockSpec(...  15.8 us
    pallas_call x2, Pallas kernels, gradient_send(): pl.pallas_call(functools.partial(gradient_send_kernel, thirds), in_specs=...  11.3 us
    pallas_call x3, Pallas kernels, combine_first(): pl.pallas_call(functools.partial(combine_first_kernel, third, has_loss),...  10.4 us
    pallas_call x1, Pallas kernels, gradient_keep(): pl.pallas_call(gradient_keep_kernel, in_specs=[pl.BlockSpec(memory_space=...  10 us
    pallas_call x1, Pallas kernels, temporal_grad_local(): pl.pallas_call(temporal_grad_kernel, in_specs=[pl.BlockSpec(memory_space=...  7.96 us
    pallas_call x1, Pallas kernels, arranged_latent(): pl.pallas_call(arrange_latent_kernel, in_specs=[pl.BlockSpec(memory_space...  5.73 us
  transfers between devices with their start and end apart: 28, of which 8 were waited for; matrix products, arithmetic and copies ran while one was open for 2% of the time, Pallas kernels for 34%

commit v1 on v0

--- a/solution.py
+++ b/solution.py
@@ -469,7 +469,7 @@
 
 
 def gradient_send_kernel(thirds, where, lat_ref, own_ref, other_ref, extra_ref, *rest):
-    outs, (pad, lat, lat_sems) = rest[: len(thirds)], rest[len(thirds) :]
+    outs, (pad, lat, lat_sems, pad_sems) = rest[: len(thirds)], rest[-4:]
     frames, span, features = own_ref.shape
     cols = pad.shape[2] // 2 - span
     height = lat.shape[1]
@@ -482,6 +482,12 @@
     for c in copies:
         c.start()
     shifted_gradient(where[0], own_ref, other_ref, pad)
+    leaving = []
+    if len(thirds) > 1:
+        pad_out = rest[len(thirds)]
+        for b in range(3):
+            leaving.append(pltpu.make_async_copy(pad.at[b], pad_out.at[b], pad_sems.at[b]))
+            leaving[b].start()
     for k, first in enumerate(thirds):
         copies[k].wait()
         start = (2 - first) * cols
@@ -491,6 +497,8 @@
                 lat[k], grad.reshape(2 * frames * span, features), preferred_element_type=F32
             ).astype(BF)
             outs[k][second, height:, :] = extra_ref[first, second * EXTRA : (second + 1) * EXTRA, :]
+    for c in leaving:
+        c.wait()
 
 
 def gradient_send(thirds, where, lat, own, other, extra, name):
@@ -503,12 +511,14 @@
     return pl.pallas_call(
         functools.partial(gradient_send_kernel, thirds),
         in_specs=[pl.BlockSpec(memory_space=pltpu.SMEM), hbm] + [vmem] * 3,
-        out_specs=[vmem] * n,
-        out_shape=[pltpu.VMEM((3, rows + EXTRA, features), BF)] * n,
+        out_specs=[vmem] * n + [hbm] * (n > 1),
+        out_shape=[pltpu.VMEM((3, rows + EXTRA, features), BF)] * n
+        + [pltpu.HBM((3, frames, 2 * span + 2 * cols, features), BF)] * (n > 1),
         scratch_shapes=[
             pltpu.VMEM((3, frames, 2 * span + 2 * cols, features), BF),
             pltpu.VMEM((n, rows, lat.shape[2]), BF),
             pltpu.SemaphoreType.DMA((n,)),
+            pltpu.SemaphoreType.DMA((3,)),
         ],
         compiler_params=params(28),
         cost_estimate=cost(1, 1),
@@ -516,57 +526,62 @@
     )(where, in_hbm(lat), own, other, in_vmem(extra))
 
 
-def gradient_keep_kernel(where, lat_ref, own_ref, other_ref, out_ref, pad, lat, lat_sems, sums, sems):
-    frames, span, features = own_ref.shape
-    cols = pad.shape[2] // 2 - span
+def gradient_keep_kernel(where, lat_ref, pad_ref, out_ref, pad, lat, lat_sems, pad_sems, sums, sems):
+    frames = pad.shape[1]
+    cols = 16
+    span = pad.shape[2] // 2 - cols
+    features = pad.shape[3]
     height = lat.shape[1]
     copies = []
     for k in range(3):
         rows = pl.ds(pl.multiple_of(where[1 + k] * height, height), height)
         copies.append(pltpu.make_async_copy(lat_ref.at[k, rows, :], lat.at[k], lat_sems.at[k]))
+    pltpu.make_async_copy(pad_ref.at[0], pad.at[0], pad_sems.at[0]).start()
     for c in copies:
         c.start()
-    shifted_gradient(where[0], own_ref, other_ref, pad)
+    for b in range(1, 3):
+        pltpu.make_async_copy(pad_ref.at[b], pad.at[b], pad_sems.at[b]).start()
     for c in copies:
         c.wait()
 
-    def one(k, carry):
-        start = pl.multiple_of((2 - k) * cols, cols)
-        for second in range(3):
-            grad = pad[second, :, pl.ds(start, 2 * span), :]
-            sums[k, second] = jnp.dot(
+    def one(b, carry):
+        pltpu.make_async_copy(pad_ref.at[b], pad.at[b], pad_sems.at[b]).wait()
+        for k in range(3):
+            start = (2 - k) * cols
+            grad = pad[b, :, start : start + 2 * span, :]
+            sums[k, b] = jnp.dot(
                 lat[k], grad.reshape(2 * frames * span, features), preferred_element_type=F32
             )
-        pltpu.make_async_copy(sums.at[k], out_ref.at[k], sems.at[k]).start()
+            pltpu.make_async_copy(sums.at[k, b], out_ref.at[k, b], sems.at[k, b]).start()
         return carry
 
     lax.fori_loop(0, 3, one, 0)
-    for k in range(3):
-        pltpu.make_async_copy(sums.at[k], out_ref.at[k], sems.at[k]).wait()
-
-
-def gradient_keep(where, lat, own, other):
-    frames, span, features = own.shape
+    for b in range(3):
+        for k in range(3):
+            pltpu.make_async_copy(sums.at[k, b], out_ref.at[k, b], sems.at[k, b]).wait()
+
+
+def gradient_keep(where, lat, pad):
+    features = pad.shape[3]
     rows = lat.shape[1] // 2
-    cols = 16
-    vmem = pl.BlockSpec(memory_space=pltpu.VMEM)
     hbm = pl.BlockSpec(memory_space=pltpu.HBM)
     return pl.pallas_call(
         gradient_keep_kernel,
-        in_specs=[pl.BlockSpec(memory_space=pltpu.SMEM), hbm, vmem, vmem],
+        in_specs=[pl.BlockSpec(memory_space=pltpu.SMEM), hbm, hbm],
         out_specs=hbm,
         out_shape=pltpu.HBM((3, 3, rows, features), F32),
         scratch_shapes=[
-            pltpu.VMEM((3, frames, 2 * span + 2 * cols, features), BF),
+            pltpu.VMEM(pad.shape, BF),
             pltpu.VMEM((3, rows, lat.shape[2]), BF),
             pltpu.SemaphoreType.DMA((3,)),
+            pltpu.SemaphoreType.DMA((3,)),
             pltpu.VMEM((3, 3, rows, features), F32),
-            pltpu.SemaphoreType.DMA((3,)),
+            pltpu.SemaphoreType.DMA((3, 3)),
         ],
         compiler_params=params(28),
         cost_estimate=cost(1, 1),
         name="spatial_keep",
-    )(where, in_hbm(lat), own, other)
+    )(where, in_hbm(lat), in_hbm(pad))
 
 
 def bit_of(value, kind):
@@ -875,9 +890,9 @@
     send_at = jnp.concatenate([core_index, 1 - first_bits])
     keep_at = jnp.concatenate([core_index, first_bits])
     (send_1,) = gradient_send((1,), send_at, lat, gh, gh_other, extra, "spatial_send_first")
-    send_2, send_0 = gradient_send((2, 0), send_at, lat, gh, gh_other, extra, "spatial_send_rest")
+    send_2, send_0, shifted = gradient_send((2, 0), send_at, lat, gh, gh_other, extra, "spatial_send_rest")
     sends = [send_0, send_1, send_2]
-    keeps = gradient_keep(keep_at, lat, gh, gh_other)
+    keeps = gradient_keep(keep_at, lat, shifted)
 
     state = [
         (sends[t].reshape(-1, features), None, more_keeps[t], loss if t == 0 else None)

time: 163 us -> 164 us (level)
  Pallas kernels: 75.1 us -> 78.2 us
  starting transfers between devices: 54.8 us -> 52.3 us
    ppermute x18, starting transfers between devices: 45 us -> 42.6 us  [on_device(): lax.ppermute(state[t][0], both, swap_pairs(ORDERS[t][step // 2], step, si...]
    unnamed x34 -> x28, local copies, waits for them, and re-layouts: 5.05 us -> 5.49 us
  transfers between devices with their start and end apart: 28 -> 28, of which waited for: 8 -> 8; matrix products, arithmetic and copies ran while one was open for 2% -> 2% of each run, Pallas kernels for 34% -> 36%
where the time goes in v1:
time: 164 us
  Pallas kernels  78.2 us (48%)
  starting transfers between devices  52.3 us (32%)
  waiting for transfers between devices  19.3 us (12%)
  local copies, waits for them, and re-layouts  5.83 us (4%)
  other arithmetic  4.73 us (3%)
  between operations  3.71 us (2%)
    ppermute x18, starting transfers between devices, on_device(): lax.ppermute(state[t][0], both, swap_pairs(ORDERS[t][step // 2], step, si...  42.6 us
    ppermute x18, waiting for transfers between devices, on_device(): lax.ppermute(state[t][0], both, swap_pairs(ORDERS[t][step // 2], step, si...  19.2 us
    pallas_call x1, Pallas kernels, spatial_forward(): pl.pallas_call(spatial_forward_kernel, grid=(3,), in_specs=[pl.BlockSpec(...  15.8 us
    pallas_call x2, Pallas kernels, gradient_send(): pl.pallas_call(functools.partial(gradient_send_kernel, thirds), in_specs=...  11.8 us
    pallas_call x1, Pallas kernels, gradient_keep(): pl.pallas_call(gradient_keep_kernel, in_specs=[pl.BlockSpec(memory_space=...  11.1 us
    pallas_call x3, Pallas kernels, combine_first(): pl.pallas_call(functools.partial(combine_first_kernel, third, has_loss),...  10.5 us
    pallas_call x1, Pallas kernels, temporal_grad_local(): pl.pallas_call(temporal_grad_kernel, in_specs=[pl.BlockSpec(memory_space=...  8.25 us
    pallas_call x1, Pallas kernels, arranged_latent(): pl.pallas_call(arrange_latent_kernel, in_specs=[pl.BlockSpec(memory_space...  5.68 us
  transfers between devices with their start and end apart: 28, of which 8 were waited for; matrix products, arithmetic and copies ran while one was open for 2% of the time, Pallas kernels for 36%

profile of v1, /device:TPU:0, one launch (start us, length us, event | category | flops | bytes accessed | tf_op | source)
XLA Modules:
  0.0 164.0 jit_solution(13521842545050135425)
XLA Ops:
  5.3 15.8 %spatial_forward.1 = (bf16[5,128,640]{2,1,0:T(8,128)(2,1)}, bf16[1,128,640]{2,1,0:T(8,128)(2,1)S(1)}, bf16[1,128,640]{2,1,0:T(8,128)(2,1)S(1)}, f32[5,128,640]{2,1,0:T(8,128)S(1)}) custom-call(s32[1]{0:T(128)} %bitcast.10.odd, bf16[5,128,1280]{2,1,0:T(8,128)(2,1)S(1)} %bitcast.104, bf16[5,16,1280]{2,1,0:T(8,128)(2,1)S(1)} %get-tuple-element.154.above_ref, ...), custom_call_target="tpu_custom_call" | custom-call | flops 9437184000 | bytes 14745600 | tf_op jit(solution)/shard_map/spatial_forward/pallas_call | solution.py:96
  25.6 2.7 %select_latent.1 = (bf16[640,640]{1,0:T(8,128)(2,1)S(1)}, bf16[640,640]{1,0:T(8,128)(2,1)S(1)}) custom-call(s32[1]{0:T(128)} %bitcast.6.core_ref, bf16[5,128,1280]{2,1,0:T(8,128)(2,1)S(1)} %bitcast.105, bf16[2,640,1280]{2,1,0:T(8,128)(2,1)S(1)} %copy-done.11, f32[5,128,640]{2,1,0:T(8,128)S(1)} %get-tuple-element.72.token.der_ref), custom_call_target="tpu_custom_call" | custom-call | flops 2097152000 | bytes 6553600 | tf_op jit(solution)/shard_map/select_latent/pallas_call | solution.py:380
  28.5 4.9 %temporal_forward.1 = (bf16[5,128,640]{2,1,0:T(8,128)(2,1)}, bf16[1,128,640]{2,1,0:T(8,128)(2,1)S(1)}, bf16[1,128,640]{2,1,0:T(8,128)(2,1)S(1)}, f32[1,640]{1,0:T(1,128)S(1)}, bf16[272,640]{1,0:T(8,128)(2,1)}) custom-call(f32[3]{0:T(128)S(1)} %pad_maximum_fusion.scale, s32[1]{0:T(128)} %bitcast.10.odd, bf16[5,128,640]{2,1,0:T(8,128)(2,1)} %get-tuple-element.75.act_ref, ...), custom_call_target="tpu_custom_call" | custom-call | flops 1572864000 | bytes 2457600 | tf_op jit(solution)/shard_map/temporal_forward/pallas_call | solution.py:166
  35.0 4.8 %collective-permute-start.4 = (bf16[1,128,640]{2,1,0:T(8,128)(2,1)}, bf16[1,128,640]{2,1,0:T(8,128)(2,1)S(1)}, u32[]{:S(2)}, u32[]{:S(2)}) collective-permute-start(bf16[1,128,640]{2,1,0:T(8,128)(2,1)} %copy-done.10), channel_id=1, source_target_pairs={{0,2},{4,6},{8,10},{12,14},{16,18},{20,22},{24,26},{28,30},{32,34}... | collective-permute-start | bytes 491528 | tf_op jit(solution)/shard_map/ppermute | solution.py:859
  40.6 8.2 %temporal_grad.1 = (bf16[3,192,640]{2,1,0:T(8,128)(2,1)S(1)}, f32[160,640]{1,0:T(8,128)}, f32[160,640]{1,0:T(8,128)}, f32[160,640]{1,0:T(8,128)}, f32[1,640]{1,0:T(1,128)S(1)}) custom-call(s32[5]{0:T(128)S(1)} %concatenate.12.bits_ref, bf16[5,128,640]{2,1,0:T(8,128)(2,1)} %get-tuple-element.75.act_ref, bf16[272,640]{1,0:T(8,128)(2,1)} %get-tuple-element.81.rim_ref, ...), custom_call_target="tpu_custom_call" | custom-call | flops 2097152000 | bytes 2457600 | tf_op jit(solution)/shard_map/temporal_grad/pallas_call | solution.py:304
  48.9 3.5 %temporal_backward.1.token.own_ref = bf16[5,128,640]{2,1,0:T(8,128)(2,1)S(1)} custom-call(s32[1]{0:T(128)} %bitcast.10.odd, bf16[5,128,640]{2,1,0:T(8,128)(2,1)} %get-tuple-element.78.gp_ref, bf16[1,128,640]{2,1,0:T(8,128)(2,1)S(1)} %collective-permute-done.4.one_ref, bf16[1,128,640]{2,1,0:T(8,128)(2,1)S(1)} %collective-permute-done.5.two_ref, ...), custom_call_target="tpu_custom_call" | custom-call | flops 1572864000 | bytes 2457600 | tf_op jit(solution)/shard_map/temporal_backward/pallas_call | solution.py:354
  52.7 5.7 %arrange_latent.1.lat_ref = bf16[3,640,1280]{2,1,0:T(8,128)(2,1)} custom-call(s32[1]{0:T(128)} %bitcast.6.core_ref, bf16[640,640]{1,0:T(8,128)(2,1)S(1)} %get-tuple-element.73.rest_0_.own_ref, bf16[640,640]{1,0:T(8,128)(2,1)S(1)} %collective-permute-done.1.other_ref, bf16[2,2,640,640]{3,2,1,0:T(8,128)(2,1)} %constant.219.clone.reorder_ref, ...), custom_call_target="tpu_custom_call" | custom-call | flops 2097152000 | bytes 8192000 | tf_op jit(solution)/shard_map/arrange_latent/pallas_call | solution.py:424
  58.4 3.9 %spatial_send_first.1 = bf16[3,384,640]{2,1,0:T(8,128)(2,1)S(1)} custom-call(s32[4]{0:T(128)S(1)} %pad_add_fusion.1.where, bf16[3,640,1280]{2,1,0:T(8,128)(2,1)} %arrange_latent.1.lat_ref, bf16[5,128,640]{2,1,0:T(8,128)(2,1)S(1)} %temporal_backward.1.token.own_ref, bf16[5,128,640]{2,1,0:T(8,128)(2,1)S(1)} %collective-permute-done.9.other_ref, ...), custom_call_target="tpu_custom_call" | custom-call | flops 1 | bytes 1 | tf_op jit(solution)/shard_map/spatial_send_first/pallas_call | solution.py:511
  62.3 8.4 %collective-permute-start.16 = (bf16[1152,640]{1,0:T(8,128)(2,1)S(1)}, bf16[1152,640]{1,0:T(8,128)(2,1)S(1)}, u32[]{:S(2)}, u32[]{:S(2)}) collective-permute-start(bf16[1152,640]{1,0:T(8,128)(2,1)S(1)} %bitcast.106), channel_id=1, source_target_pairs={{0,8},{1,25},{2,10},{3,27},{4,12},{5,29},{6,14},{7,31},{8,0},{9,17... | collective-permute-start | bytes 4423688 | tf_op jit(solution)/shard_map/ppermute | solution.py:904
  70.7 8.0 %spatial_send_rest.1 = (bf16[3,384,640]{2,1,0:T(8,128)(2,1)}, bf16[3,384,640]{2,1,0:T(8,128)(2,1)}, bf16[3,5,288,640]{3,2,1,0:T(8,128)(2,1)}) custom-call(s32[4]{0:T(128)S(1)} %pad_add_fusion.1.where, bf16[3,640,1280]{2,1,0:T(8,128)(2,1)} %arrange_latent.1.lat_ref, bf16[5,128,640]{2,1,0:T(8,128)(2,1)S(1)} %temporal_backward.1.token.own_ref, ...), custom_call_target="tpu_custom_call" | custom-call | flops 1 | bytes 1 | tf_op jit(solution)/shard_map/spatial_send_rest/pallas_call | solution.py:511
  78.7 4.7 %collective-permute-start.10 = (bf16[1152,640]{1,0:T(8,128)(2,1)}, bf16[1152,640]{1,0:T(8,128)(2,1)}, u32[]{:S(2)}, u32[]{:S(2)}) collective-permute-start(bf16[1152,640]{1,0:T(8,128)(2,1)} %bitcast.18), channel_id=1, source_target_pairs={{0,32},{1,97},{2,34},{3,99},{4,36},{5,101},{6,38},{7,103},{8,40},{... | collective-permute-start | bytes 4423688 | tf_op jit(solution)/shard_map/ppermute | solution.py:904
  83.5 11.1 %spatial_keep.1.keep_ref = f32[3,3,320,640]{3,2,1,0:T(8,128)} custom-call(s32[4]{0:T(128)S(1)} %pad_add_fusion.where, bf16[3,640,1280]{2,1,0:T(8,128)(2,1)} %arrange_latent.1.lat_ref, bf16[3,5,288,640]{3,2,1,0:T(8,128)(2,1)} %get-tuple-element.85.pad_ref), custom_call_target="tpu_custom_call" | custom-call | flops 1 | bytes 1 | tf_op jit(solution)/shard_map/spatial_keep/pallas_call | solution.py:568
  95.9 3.8 %combine_0_1.1 = (bf16[560,640]{1,0:T(8,128)(2,1)}, f32[3,160,640]{2,1,0:T(8,128)S(1)}, f32[80,640]{1,0:T(8,128)S(1)}) custom-call(s32[6]{0:T(128)S(1)} %stack.112.bits, f32[3,3,320,640]{3,2,1,0:T(8,128)} %spatial_keep.1.keep_ref, bf16[3,384,640]{2,1,0:T(8,128)(2,1)} %bitcast.107, f32[160,640]{1,0:T(8,128)} %get-tuple-element.107.tp_ref), custom_call_target="tpu_custom_call" | custom-call | bytes 1638400 | tf_op jit(solution)/shard_map/combine_0_1/pallas_call | solution.py:731
  99.9 3.8 %combine_0_2.1 = (bf16[560,640]{1,0:T(8,128)(2,1)}, f32[3,160,640]{2,1,0:T(8,128)S(1)}, f32[80,640]{1,0:T(8,128)S(1)}) custom-call(s32[6]{0:T(128)S(1)} %stack.118.bits, f32[3,3,320,640]{3,2,1,0:T(8,128)} %spatial_keep.1.keep_ref, bf16[3,384,640]{2,1,0:T(8,128)(2,1)} %bitcast.37.met_ref, f32[160,640]{1,0:T(8,128)} %get-tuple-element.123.tp_ref), custom_call_target="tpu_custom_call" | custom-call | bytes 1638400 | tf_op jit(solution)/shard_map/combine_0_2/pallas_call | solution.py:731
  107.0 3.0 %combine_0_0.1 = (bf16[576,640]{1,0:T(8,128)(2,1)S(1)}, f32[3,160,640]{2,1,0:T(8,128)S(1)}, f32[80,640]{1,0:T(8,128)S(1)}, f32[1,640]{1,0:T(1,128)S(1)}) custom-call(s32[6]{0:T(128)S(1)} %stack.104.bits, f32[3,3,320,640]{3,2,1,0:T(8,128)} %spatial_keep.1.keep_ref, bf16[3,384,640]{2,1,0:T(8,128)(2,1)} %bitcast.19.met_ref, ...), custom_call_target="tpu_custom_call" | custom-call | bytes 1638400 | tf_op jit(solution)/shard_map/combine_0_0/pallas_call | solution.py:731
  114.8 2.8 %collective-permute-done.23.met_ref = bf16[560,640]{1,0:T(8,128)(2,1)} collective-permute-done((bf16[560,640]{1,0:T(8,128)(2,1)}, bf16[560,640]{1,0:T(8,128)(2,1)}, u32[]{:S(2)}, u32[]{:S(2)}) %collective-permute-start.23) | collective-permute-done | bytes 716832 | tf_op jit(solution)/shard_map/ppermute | solution.py:904
  119.0 4.4 %collective-permute-start.24 = (bf16[288,640]{1,0:T(8,128)(2,1)S(1)}, bf16[288,640]{1,0:T(8,128)(2,1)S(1)}, u32[]{:S(2)}, u32[]{:S(2)}) collective-permute-start(bf16[288,640]{1,0:T(8,128)(2,1)S(1)} %get-tuple-element.127), channel_id=1, source_target_pairs={{0,32},{1,97},{2,34},{3,99},{4,36},{5,101},{6,38},{7,103},{8,40},{... | collective-permute-start | bytes 1105928 | tf_op jit(solution)/shard_map/ppermute | solution.py:904
  123.8 4.2 %collective-permute-start.12 = (bf16[304,640]{1,0:T(8,128)(2,1)S(1)}, bf16[304,640]{1,0:T(8,128)(2,1)S(1)}, u32[]{:S(2)}, u32[]{:S(2)}) collective-permute-start(bf16[304,640]{1,0:T(8,128)(2,1)S(1)} %get-tuple-element.92), channel_id=1, source_target_pairs={{0,8},{1,25},{2,10},{3,27},{4,12},{5,29},{6,14},{7,31},{8,0},{9,17... | collective-permute-start | bytes 1167368 | tf_op jit(solution)/shard_map/ppermute | solution.py:904
  130.4 3.8 %collective-permute-start.25 = (bf16[176,640]{1,0:T(8,128)(2,1)S(1)}, bf16[176,640]{1,0:T(8,128)(2,1)S(1)}, u32[]{:S(2)}, u32[]{:S(2)}) collective-permute-start(bf16[176,640]{1,0:T(8,128)(2,1)S(1)} %get-tuple-element.130), channel_id=1, source_target_pairs={{0,96},{1,33},{2,98},{3,35},{4,100},{5,37},{6,102},{7,39},{8,104},... | collective-permute-start | bytes 675848 | tf_op jit(solution)/shard_map/ppermute | solution.py:904
  135.8 3.0 %collective-permute-done.25.met_ref = bf16[176,640]{1,0:T(8,128)(2,1)S(1)} collective-permute-done((bf16[176,640]{1,0:T(8,128)(2,1)S(1)}, bf16[176,640]{1,0:T(8,128)(2,1)S(1)}, u32[]{:S(2)}, u32[]{:S(2)}) %collective-permute-start.25) | collective-permute-done | bytes 225312 | tf_op jit(solution)/shard_map/ppermute | solution.py:904
  139.0 5.2 %collective-permute-start.26 = (bf16[112,640]{1,0:T(8,128)(2,1)S(1)}, bf16[112,640]{1,0:T(8,128)(2,1)S(1)}, u32[]{:S(2)}, u32[]{:S(2)}) collective-permute-start(bf16[112,640]{1,0:T(8,128)(2,1)S(1)} %get-tuple-element.133), channel_id=1, source_target_pairs={{0,8},{1,25},{2,10},{3,27},{4,12},{5,29},{6,14},{7,31},{8,0},{9,17... | collective-permute-start | bytes 430088 | tf_op jit(solution)/shard_map/ppermute | solution.py:904
  144.3 2.8 %collective-permute-start.21 = (bf16[64,640]{1,0:T(8,128)(2,1)S(1)}, bf16[64,640]{1,0:T(8,128)(2,1)S(1)}, u32[]{:S(2)}, u32[]{:S(2)}) collective-permute-start(bf16[64,640]{1,0:T(8,128)(2,1)S(1)} %get-tuple-element.121), channel_id=1, source_target_pairs={{0,96},{1,33},{2,98},{3,35},{4,100},{5,37},{6,102},{7,39},{8,104},... | collective-permute-start | bytes 245768 | tf_op jit(solution)/shard_map/ppermute | solution.py:904
  150.1 3.9 %collective-permute-done.27 = bf16[64,640]{1,0:T(8,128)(2,1)S(1)} collective-permute-done((bf16[64,640]{1,0:T(8,128)(2,1)S(1)}, bf16[64,640]{1,0:T(8,128)(2,1)S(1)}, u32[]{:S(2)}, u32[]{:S(2)}) %collective-permute-start.27) | collective-permute-done | bytes 81952 | tf_op jit(solution)/shard_map/ppermute | solution.py:904
  154.2 5.8 %collective-permute-done.15 = bf16[80,640]{1,0:T(8,128)(2,1)S(1)} collective-permute-done((bf16[80,640]{1,0:T(8,128)(2,1)S(1)}, bf16[80,640]{1,0:T(8,128)(2,1)S(1)}, u32[]{:S(2)}, u32[]{:S(2)}) %collective-permute-start.15) | collective-permute-done | bytes 102432 | tf_op jit(solution)/shard_map/ppermute | solution.py:904
  (107 shorter events, 32.0 us)
Async XLA Ops:
  21.2 7.2 %collective-permute-start.2 = (bf16[1,128,640]{2,1,0:T(8,128)(2,1)S(1)}, bf16[1,128,640]{2,1,0:T(8,128)(2,1)S(1)}, u32[]{:S(2)}, u32[]{:S(2)}) collective-permute-start(bf16[1,128,640]{2,1,0:T(8,128)(2,1)S(1)} %get-tuple-element.76), channel_id=1, source_target_pairs={{0,2},{4,6},{8,10},{12,14},{16,18},{20,22},{24,26},{28,30},{32,34}... | collective-permute-start | bytes 491528 | tf_op jit(solution)/shard_map/ppermute | solution.py:840
  23.9 16.7 %collective-permute-start.6 = (bf16[5,128,640]{2,1,0:T(8,128)(2,1)}, bf16[5,128,640]{2,1,0:T(8,128)(2,1)}, u32[]{:S(2)}, u32[]{:S(2)}) collective-permute-start(bf16[5,128,640]{2,1,0:T(8,128)(2,1)} %get-tuple-element.75.act_ref), channel_id=1, source_target_pairs={{0,1},{1,0},{2,3},{3,2},{4,5},{5,4},{6,7},{7,6},{8,9},{9,8},{10,11... | collective-permute-start | bytes 2457608 | tf_op jit(solution)/shard_map/ppermute | solution.py:842
  34.1 6.5 %collective-permute-start.8 = (bf16[5,128,640]{2,1,0:T(8,128)(2,1)}, bf16[5,128,640]{2,1,0:T(8,128)(2,1)}, u32[]{:S(2)}, u32[]{:S(2)}) collective-permute-start(bf16[5,128,640]{2,1,0:T(8,128)(2,1)} %get-tuple-element.78.gp_ref), channel_id=1, source_target_pairs={{0,1},{1,0},{2,3},{3,2},{4,5},{5,4},{6,7},{7,6},{8,9},{9,8},{10,11... | collective-permute-start | bytes 2457608 | tf_op jit(solution)/shard_map/ppermute | solution.py:861
  34.6 18.0 %collective-permute-start.1 = (bf16[640,640]{1,0:T(8,128)(2,1)}, bf16[640,640]{1,0:T(8,128)(2,1)S(1)}, u32[]{:S(2)}, u32[]{:S(2)}) collective-permute-start(bf16[640,640]{1,0:T(8,128)(2,1)} %copy-done.9), channel_id=1, source_target_pairs={{0,1},{1,0},{2,3},{3,2},{4,5},{5,4},{6,7},{7,6},{8,9},{9,8},{10,11... | collective-permute-start | bytes 2457608 | tf_op jit(solution)/shard_map/ppermute | solution.py:846
  35.0 13.9 %collective-permute-start.4 = (bf16[1,128,640]{2,1,0:T(8,128)(2,1)}, bf16[1,128,640]{2,1,0:T(8,128)(2,1)S(1)}, u32[]{:S(2)}, u32[]{:S(2)}) collective-permute-start(bf16[1,128,640]{2,1,0:T(8,128)(2,1)} %copy-done.10), channel_id=1, source_target_pairs={{0,2},{4,6},{8,10},{12,14},{16,18},{20,22},{24,26},{28,30},{32,34}... | collective-permute-start | bytes 491528 | tf_op jit(solution)/shard_map/ppermute | solution.py:859
  39.7 9.1 %collective-permute-start.5 = (bf16[1,128,640]{2,1,0:T(8,128)(2,1)S(1)}, bf16[1,128,640]{2,1,0:T(8,128)(2,1)S(1)}, u32[]{:S(2)}, u32[]{:S(2)}) collective-permute-start(bf16[1,128,640]{2,1,0:T(8,128)(2,1)S(1)} %get-tuple-element.80), channel_id=1, source_target_pairs={{2,4},{6,8},{10,12},{14,16},{18,20},{26,28},{30,32},{34,36},{38,40... | collective-permute-start | bytes 491528 | tf_op jit(solution)/shard_map/ppermute | solution.py:860
  52.4 5.9 %collective-permute-start.9 = (bf16[5,128,640]{2,1,0:T(8,128)(2,1)S(1)}, bf16[5,128,640]{2,1,0:T(8,128)(2,1)S(1)}, u32[]{:S(2)}, u32[]{:S(2)}) collective-permute-start(bf16[5,128,640]{2,1,0:T(8,128)(2,1)S(1)} %temporal_backward.1.token.own_ref), channel_id=1, source_target_pairs={{0,1},{1,0},{2,3},{3,2},{4,5},{5,4},{6,7},{7,6},{8,9},{9,8},{10,11... | collective-permute-start | bytes 2457608 | tf_op jit(solution)/shard_map/ppermute | solution.py:886
  62.3 32.4 %collective-permute-start.16 = (bf16[1152,640]{1,0:T(8,128)(2,1)S(1)}, bf16[1152,640]{1,0:T(8,128)(2,1)S(1)}, u32[]{:S(2)}, u32[]{:S(2)}) collective-permute-start(bf16[1152,640]{1,0:T(8,128)(2,1)S(1)} %bitcast.106), channel_id=1, source_target_pairs={{0,8},{1,25},{2,10},{3,27},{4,12},{5,29},{6,14},{7,31},{8,0},{9,17... | collective-permute-start | bytes 4423688 | tf_op jit(solution)/shard_map/ppermute | solution.py:904
  78.6 21.3 %collective-permute-start.22 = (bf16[1152,640]{1,0:T(8,128)(2,1)}, bf16[1152,640]{1,0:T(8,128)(2,1)}, u32[]{:S(2)}, u32[]{:S(2)}) collective-permute-start(bf16[1152,640]{1,0:T(8,128)(2,1)} %bitcast.36), channel_id=1, source_target_pairs={{0,2},{1,7},{2,0},{3,5},{4,6},{5,3},{6,4},{7,1},{8,10},{9,15},{10,... | collective-permute-start | bytes 4423688 | tf_op jit(solution)/shard_map/ppermute | solution.py:904
  78.7 28.2 %collective-permute-start.10 = (bf16[1152,640]{1,0:T(8,128)(2,1)}, bf16[1152,640]{1,0:T(8,128)(2,1)}, u32[]{:S(2)}, u32[]{:S(2)}) collective-permute-start(bf16[1152,640]{1,0:T(8,128)(2,1)} %bitcast.18), channel_id=1, source_target_pairs={{0,32},{1,97},{2,34},{3,99},{4,36},{5,101},{6,38},{7,103},{8,40},{... | collective-permute-start | bytes 4423688 | tf_op jit(solution)/shard_map/ppermute | solution.py:904
  99.7 12.7 %collective-permute-start.17 = (bf16[560,640]{1,0:T(8,128)(2,1)}, bf16[560,640]{1,0:T(8,128)(2,1)S(1)}, u32[]{:S(2)}, u32[]{:S(2)}) collective-permute-start(bf16[560,640]{1,0:T(8,128)(2,1)} %get-tuple-element.108), channel_id=1, source_target_pairs={{0,24},{1,9},{2,26},{3,11},{4,28},{5,13},{6,30},{7,15},{8,16},{9,1... | collective-permute-start | bytes 2150408 | tf_op jit(solution)/shard_map/ppermute | solution.py:904
  104.4 13.2 %collective-permute-start.23 = (bf16[560,640]{1,0:T(8,128)(2,1)}, bf16[560,640]{1,0:T(8,128)(2,1)}, u32[]{:S(2)}, u32[]{:S(2)}) collective-permute-start(bf16[560,640]{1,0:T(8,128)(2,1)} %get-tuple-element.124), channel_id=1, source_target_pairs={{0,6},{1,3},{2,4},{3,1},{4,2},{5,7},{6,0},{7,5},{8,14},{9,11},{10,... | collective-permute-start | bytes 2150408 | tf_op jit(solution)/shard_map/ppermute | solution.py:904
  109.9 13.5 %collective-permute-start.11 = (bf16[576,640]{1,0:T(8,128)(2,1)S(1)}, bf16[576,640]{1,0:T(8,128)(2,1)S(1)}, u32[]{:S(2)}, u32[]{:S(2)}) collective-permute-start(bf16[576,640]{1,0:T(8,128)(2,1)S(1)} %get-tuple-element.88), channel_id=1, source_target_pairs={{0,96},{1,33},{2,98},{3,35},{4,100},{5,37},{6,102},{7,39},{8,104},... | collective-permute-start | bytes 2211848 | tf_op jit(solution)/shard_map/ppermute | solution.py:904
  112.8 15.2 %collective-permute-start.18 = (bf16[288,640]{1,0:T(8,128)(2,1)S(1)}, bf16[288,640]{1,0:T(8,128)(2,1)S(1)}, u32[]{:S(2)}, u32[]{:S(2)}) collective-permute-start(bf16[288,640]{1,0:T(8,128)(2,1)S(1)} %get-tuple-element.111), channel_id=1, source_target_pairs={{0,2},{1,7},{2,0},{3,5},{4,6},{5,3},{6,4},{7,1},{8,10},{9,15},{10,... | collective-permute-start | bytes 1105928 | tf_op jit(solution)/shard_map/ppermute | solution.py:904
  119.0 11.0 %collective-permute-start.24 = (bf16[288,640]{1,0:T(8,128)(2,1)S(1)}, bf16[288,640]{1,0:T(8,128)(2,1)S(1)}, u32[]{:S(2)}, u32[]{:S(2)}) collective-permute-start(bf16[288,640]{1,0:T(8,128)(2,1)S(1)} %get-tuple-element.127), channel_id=1, source_target_pairs={{0,32},{1,97},{2,34},{3,99},{4,36},{5,101},{6,38},{7,103},{8,40},{... | collective-permute-start | bytes 1105928 | tf_op jit(solution)/shard_map/ppermute | solution.py:904
  123.8 10.5 %collective-permute-start.12 = (bf16[304,640]{1,0:T(8,128)(2,1)S(1)}, bf16[304,640]{1,0:T(8,128)(2,1)S(1)}, u32[]{:S(2)}, u32[]{:S(2)}) collective-permute-start(bf16[304,640]{1,0:T(8,128)(2,1)S(1)} %get-tuple-element.92), channel_id=1, source_target_pairs={{0,8},{1,25},{2,10},{3,27},{4,12},{5,29},{6,14},{7,31},{8,0},{9,17... | collective-permute-start | bytes 1167368 | tf_op jit(solution)/shard_map/ppermute | solution.py:904
  128.3 7.3 %collective-permute-start.19 = (bf16[176,640]{1,0:T(8,128)(2,1)S(1)}, bf16[176,640]{1,0:T(8,128)(2,1)S(1)}, u32[]{:S(2)}, u32[]{:S(2)}) collective-permute-start(bf16[176,640]{1,0:T(8,128)(2,1)S(1)} %get-tuple-element.114), channel_id=1, source_target_pairs={{0,6},{1,3},{2,4},{3,1},{4,2},{5,7},{6,0},{7,5},{8,14},{9,11},{10,... | collective-permute-start | bytes 675848 | tf_op jit(solution)/shard_map/ppermute | solution.py:904
  130.4 8.5 %collective-permute-start.25 = (bf16[176,640]{1,0:T(8,128)(2,1)S(1)}, bf16[176,640]{1,0:T(8,128)(2,1)S(1)}, u32[]{:S(2)}, u32[]{:S(2)}) collective-permute-start(bf16[176,640]{1,0:T(8,128)(2,1)S(1)} %get-tuple-element.130), channel_id=1, source_target_pairs={{0,96},{1,33},{2,98},{3,35},{4,100},{5,37},{6,102},{7,39},{8,104},... | collective-permute-start | bytes 675848 | tf_op jit(solution)/shard_map/ppermute | solution.py:904
  134.6 12.6 %collective-permute-start.13 = (bf16[192,640]{1,0:T(8,128)(2,1)S(1)}, bf16[192,640]{1,0:T(8,128)(2,1)S(1)}, u32[]{:S(2)}, u32[]{:S(2)}) collective-permute-start(bf16[192,640]{1,0:T(8,128)(2,1)S(1)} %get-tuple-element.96), channel_id=1, source_target_pairs={{0,24},{1,9},{2,26},{3,11},{4,28},{5,13},{6,30},{7,15},{8,16},{9,1... | collective-permute-start | bytes 737288 | tf_op jit(solution)/shard_map/ppermute | solution.py:904
  135.7 8.5 %collective-permute-start.20 = (bf16[112,640]{1,0:T(8,128)(2,1)S(1)}, bf16[112,640]{1,0:T(8,128)(2,1)S(1)}, u32[]{:S(2)}, u32[]{:S(2)}) collective-permute-start(bf16[112,640]{1,0:T(8,128)(2,1)S(1)} %get-tuple-element.117), channel_id=1, source_target_pairs={{0,32},{1,97},{2,34},{3,99},{4,36},{5,101},{6,38},{7,103},{8,40},{... | collective-permute-start | bytes 430088 | tf_op jit(solution)/shard_map/ppermute | solution.py:904
  139.0 9.1 %collective-permute-start.26 = (bf16[112,640]{1,0:T(8,128)(2,1)S(1)}, bf16[112,640]{1,0:T(8,128)(2,1)S(1)}, u32[]{:S(2)}, u32[]{:S(2)}) collective-permute-start(bf16[112,640]{1,0:T(8,128)(2,1)S(1)} %get-tuple-element.133), channel_id=1, source_target_pairs={{0,8},{1,25},{2,10},{3,27},{4,12},{5,29},{6,14},{7,31},{8,0},{9,17... | collective-permute-start | bytes 430088 | tf_op jit(solution)/shard_map/ppermute | solution.py:904
  144.3 5.7 %collective-permute-start.21 = (bf16[64,640]{1,0:T(8,128)(2,1)S(1)}, bf16[64,640]{1,0:T(8,128)(2,1)S(1)}, u32[]{:S(2)}, u32[]{:S(2)}) collective-permute-start(bf16[64,640]{1,0:T(8,128)(2,1)S(1)} %get-tuple-element.121), channel_id=1, source_target_pairs={{0,96},{1,33},{2,98},{3,35},{4,100},{5,37},{6,102},{7,39},{8,104},... | collective-permute-start | bytes 245768 | tf_op jit(solution)/shard_map/ppermute | solution.py:904
  147.3 6.7 %collective-permute-start.14 = (bf16[128,640]{1,0:T(8,128)(2,1)S(1)}, bf16[128,640]{1,0:T(8,128)(2,1)S(1)}, u32[]{:S(2)}, u32[]{:S(2)}) collective-permute-start(bf16[128,640]{1,0:T(8,128)(2,1)S(1)} %get-tuple-element.100), channel_id=1, source_target_pairs={{0,2},{1,7},{2,0},{3,5},{4,6},{5,3},{6,4},{7,1},{8,10},{9,15},{10,... | collective-permute-start | bytes 491528 | tf_op jit(solution)/shard_map/ppermute | solution.py:904
  154.1 6.0 %collective-permute-start.15 = (bf16[80,640]{1,0:T(8,128)(2,1)S(1)}, bf16[80,640]{1,0:T(8,128)(2,1)S(1)}, u32[]{:S(2)}, u32[]{:S(2)}) collective-permute-start(bf16[80,640]{1,0:T(8,128)(2,1)S(1)} %get-tuple-element.105), channel_id=1, source_target_pairs={{0,6},{1,3},{2,4},{3,1},{4,2},{5,7},{6,0},{7,5},{8,14},{9,11},{10,... | collective-permute-start | bytes 307208 | tf_op jit(solution)/shard_map/ppermute | solution.py:904
  (17 other events, 94.4 us)
